TPU v7x, 128 devices: a whole 4x4x4 slice. The times are simulated.
128 devices in a mesh: dp: 4 (over z), section: 2 (over core), seq: 16 (over x, y).
Axes of the slice: x: 4, y: 4, z: 4, core: 2. Of those that a mesh axis runs over, the one named last changes fastest.
Arguments:
- inputs: bfloat16 [2, 4, 2048, 1024], P(None, 'dp', 'seq'), may hold values from -6 to 6
- out_grad: bfloat16 [2, 4, 2048, 1024], P(None, 'dp', 'seq'), may hold values from -6 to 6
- norm_gain: bfloat16 [2, 1024], P('section', ('dp', 'seq')), may hold values from 0.5 to 1.5
- w_in: bfloat16 [2, 1024, 4384], P('section', ('dp', 'seq')), may hold values from -0.1875 to 0.1875
- conv_w: bfloat16 [2, 4, 2304], P('section', None, ('dp', 'seq')), may hold values from -3 to 3
- conv_b: bfloat16 [2, 2304], P('section', ('dp', 'seq')), may hold values from -3 to 3
- dt_bias: float32 [2, 32], P('section'), may hold values from -7 to -3
- a_log: float32 [2, 32], P('section'), may hold values from -1 to 2
- d_skip: float32 [2, 32], P('section'), may hold values from 0.25 to 1
- gnorm_gain: bfloat16 [2, 2048], P('section', ('dp', 'seq')), may hold values from 0.5 to 1.5
- w_out: bfloat16 [2, 2048, 1024], P('section', ('dp', 'seq')), may hold values from -0.125 to 0.125
Outputs:
- outputs: bfloat16 [2, 4, 2048, 1024], P(None, 'dp', 'seq', 'section')
- in_grad: float32 [2, 4, 2048, 1024], P(None, 'dp', 'seq', 'section')
- grad_norm_gain: float32 [2, 1024], P('section', ('dp', 'seq'))
- grad_w_in: float32 [2, 1024, 4384], P('section', ('dp', 'seq'))
- grad_conv_w: float32 [2, 4, 2304], P('section', None, ('dp', 'seq'))
- grad_conv_b: float32 [2, 2304], P('section', ('dp', 'seq'))
- grad_dt_bias: float32 [2, 32], P('section')
- grad_a_log: float32 [2, 32], P('section')
- grad_d_skip: float32 [2, 32], P('section')
- grad_gnorm_gain: float32 [2, 2048], P('section', ('dp', 'seq'))
- grad_w_out: float32 [2, 2048, 1024], P('section', ('dp', 'seq'))
All inputs are finite; a program needn't handle non-finite values.
Results may differ from a plain program's by a relative error of at most 0.035.
Values may be sent and summed in bfloat16 or wider, within the bound.
No kernel may reach another device: no remote copies, remote signals or barrier semaphores. Data moves between devices by JAX's collectives and lax.ppermute only.
A program may use at most 256 MiB of HBM per device.

v0:
```python
import jax
import jax.numpy as jnp
from jax import lax
from jax.sharding import PartitionSpec as P

DIN = 2048
HEADS = 32
HEADDIM = 64
STATE = 128
KW = 4
STRETCH = 256


epsilon = 1e-05
highest = lax.Precision.HIGHEST


def passed_along(value, axis, steps):
    count = lax.axis_size(axis)
    leading, last = (max(0, -steps), min(count, count - steps))
    return lax.ppermute(value, axis, [(source, source + steps) for source in range(leading, last)])


def from_partner(value, axis, distance):
    return lax.ppermute(value, axis, [(i, i ^ 1 << distance) for i in range(lax.axis_size(axis))])


def causal_conv(values, kernel, offsets):
    taps = kernel.shape[0]
    length = values.shape[0]
    padded = jnp.pad(values, ((taps - 1, 0), (0, 0)))
    summed = offsets[None, :] + kernel[0][None, :] * padded[0:length]
    for tap_index in range(1, taps):
        summed = summed + kernel[tap_index][None, :] * padded[tap_index : tap_index + length]
    return summed


def state_space(inputs_x, delta, rate, keys_b, queries_c, block):
    length, heads, width = inputs_x.shape
    states = keys_b.shape[1]
    blocks = length // block
    values = inputs_x.reshape(blocks, block, heads, width)
    deltas = delta.reshape(blocks, block, heads)
    keys = keys_b.reshape(blocks, block, states)
    queries = queries_c.reshape(blocks, block, states)
    cumulative = jnp.cumsum(deltas * rate[None, None, :], axis=1)
    scores = jnp.einsum("cln,csn->cls", queries, keys, precision=highest)
    row_ids = lax.broadcasted_iota(jnp.int32, (block, block), 0)
    column_ids = lax.broadcasted_iota(jnp.int32, (block, block), 1)
    causal = (row_ids >= column_ids)[None, :, :, None]
    log_gaps = cumulative[:, :, None, :] - cumulative[:, None, :, :]
    decays = jnp.where(causal, jnp.exp(jnp.where(causal, log_gaps, 0.0)), 0.0)
    mixing = scores[:, :, :, None] * decays * deltas[:, None, :, :]
    within = jnp.einsum("clsh,cshp->clhp", mixing, values, precision=highest)
    to_end = jnp.exp(cumulative[:, -1:, :] - cumulative) * deltas
    block_states = jnp.einsum(
        "csn,cshp->chnp", keys, to_end[:, :, :, None] * values, precision=highest
    )
    totals = jnp.exp(cumulative[:, -1, :])

    def carry_step(carried, pieces):
        factor, added = pieces
        return (factor[:, None, None] * carried + added, carried)

    initial = jnp.zeros((heads, states, width), inputs_x.dtype)
    _, entering = lax.scan(carry_step, initial, (totals, block_states))
    across = (
        jnp.einsum("cln,chnp->clhp", queries, entering, precision=highest)
        * jnp.exp(cumulative)[:, :, :, None]
    )
    return (within + across).reshape(length, heads, width)


def mixer(x_raw, dt_raw, bc_raw, x_kernel, x_offset, bc_kernel, bc_offset, bias, log_rate, skip):
    length = x_raw.shape[0]
    heads = dt_raw.shape[1]
    x_conv = jax.nn.silu(causal_conv(x_raw, x_kernel, x_offset))
    bc_conv = jax.nn.silu(causal_conv(bc_raw, bc_kernel, bc_offset))
    states = bc_conv.shape[1] // 2
    delta = jax.nn.softplus(dt_raw + bias[None, :])
    rate = -jnp.exp(log_rate)
    inputs_x = x_conv.reshape(length, heads, -1)
    result = state_space(inputs_x, delta, rate, bc_conv[:, :states], bc_conv[:, states:], STRETCH)
    result = result + skip[None, :, None] * inputs_x
    return result.reshape(length, -1)


def pre_norm(stream, gain):
    inverse_rms = lax.rsqrt(jnp.mean(stream * stream, axis=-1, keepdims=True) + epsilon)
    return stream * inverse_rms * gain[None, :]


def post_norm(mixed, gate_part, gain):
    gated = mixed * jax.nn.silu(gate_part)
    inverse_rms = lax.rsqrt(jnp.mean(gated * gated, axis=-1, keepdims=True) + epsilon)
    return gated * inverse_rms * gain[None, :]


def contract_rows(left, right):
    return lax.dot_general(
        left, right, (((0,), (0,)), ((), ())), preferred_element_type=jnp.float32
    )


def contract_cols(left, right):
    return lax.dot_general(
        left, right, (((1,), (1,)), ((), ())), preferred_element_type=jnp.float32
    )


def local_params(weights, head_params, group, heads_dev):
    width_dev = heads_dev * HEADDIM
    kernel = weights[2].astype(jnp.float32)
    offsets = weights[3].astype(jnp.float32)
    x_kernel = lax.dynamic_slice_in_dim(kernel, group * width_dev, width_dev, 1)
    x_offset = lax.dynamic_slice_in_dim(offsets, group * width_dev, width_dev, 0)
    picked = tuple(
        (
            lax.dynamic_slice_in_dim(values, group * heads_dev, heads_dev, 0)
            for values in head_params
        )
    )
    return (x_kernel, x_offset, kernel[:, DIN:], offsets[DIN:], picked[0], picked[1], picked[2])


def forward_layer(stream, weights, mix_params):
    hidden = pre_norm(stream, weights[0].astype(jnp.float32)).astype(jnp.bfloat16)
    projected = jnp.dot(hidden, weights[1], preferred_element_type=jnp.float32).astype(jnp.bfloat16)
    gate_part = projected[:, :DIN]
    x_raw = projected[:, DIN : 2 * DIN]
    bc_raw = projected[:, 2 * DIN : 2 * DIN + 2 * STATE]
    dt_raw = projected[:, 2 * DIN + 2 * STATE :]
    x_heads, dt_heads = (
        lax.all_to_all(x_raw, "seq", split_axis=1, concat_axis=0, tiled=True),
        lax.all_to_all(dt_raw, "seq", split_axis=1, concat_axis=0, tiled=True),
    )
    bc_whole = lax.all_gather(bc_raw, "seq", axis=0, tiled=True)
    mixed = mixer(
        x_heads.astype(jnp.float32),
        dt_heads.astype(jnp.float32),
        bc_whole.astype(jnp.float32),
        *mix_params
    ).astype(jnp.bfloat16)
    mixed_seq = lax.all_to_all(mixed, "seq", split_axis=0, concat_axis=1, tiled=True)
    normed = post_norm(
        mixed_seq.astype(jnp.float32), gate_part.astype(jnp.float32), weights[4].astype(jnp.float32)
    ).astype(jnp.bfloat16)
    result = stream + jnp.dot(normed, weights[5], preferred_element_type=jnp.float32)
    return ((stream, hidden, projected, x_heads, dt_heads, bc_whole, mixed_seq), result)


def back_top(kept, upstream, weights):
    projected = kept[2]
    mixed_seq = kept[6]
    gate_float = projected[:, :DIN].astype(jnp.float32)
    gnorm_float = weights[4].astype(jnp.float32)
    mixed_float = mixed_seq.astype(jnp.float32)
    normed = post_norm(mixed_float, gate_float, gnorm_float).astype(jnp.bfloat16)
    upstream_low = upstream.astype(jnp.bfloat16)
    out_weight_grad = contract_rows(normed, upstream_low)
    normed_grad = contract_cols(upstream_low, weights[5])
    _, post_back = jax.vjp(post_norm, mixed_float, gate_float, gnorm_float)
    mixed_grad, gate_grad, gnorm_grad = post_back(normed_grad)
    return (out_weight_grad, gnorm_grad, mixed_grad, gate_grad)


def back_bottom(kept, upstream, weights, mix_params, group, heads_dev, mixed_grad, gate_grad):
    stream, hidden, projected, x_heads, dt_heads, bc_whole, mixed_seq = kept
    heads_grad = lax.all_to_all(
        mixed_grad.astype(jnp.bfloat16), "seq", split_axis=1, concat_axis=0, tiled=True
    )
    _, mixer_back = jax.vjp(
        mixer,
        x_heads.astype(jnp.float32),
        dt_heads.astype(jnp.float32),
        bc_whole.astype(jnp.float32),
        *mix_params
    )
    (
        x_grad,
        dt_grad,
        bc_grad,
        xk_grad,
        xo_grad,
        bck_grad,
        bco_grad,
        bias_grad,
        rate_grad,
        skip_grad,
    ) = mixer_back(heads_grad.astype(jnp.float32))
    x_back, dt_back = (
        lax.all_to_all(x_grad.astype(jnp.bfloat16), "seq", split_axis=0, concat_axis=1, tiled=True),
        lax.all_to_all(
            dt_grad.astype(jnp.bfloat16), "seq", split_axis=0, concat_axis=1, tiled=True
        ),
    )
    bc_back = lax.psum_scatter(
        bc_grad.astype(jnp.bfloat16), "seq", scatter_dimension=0, tiled=True
    ).astype(jnp.float32)
    proj_grad = jnp.concatenate(
        [gate_grad, x_back.astype(jnp.float32), bc_back, dt_back.astype(jnp.float32)], axis=1
    ).astype(jnp.bfloat16)
    in_weight_grad = contract_rows(hidden, proj_grad)
    hidden_grad = contract_cols(proj_grad, weights[1])
    _, pre_back = jax.vjp(pre_norm, stream, weights[0].astype(jnp.float32))
    stream_grad, norm_grad = pre_back(hidden_grad)
    width_dev = heads_dev * HEADDIM
    conv_w_grad = jnp.concatenate(
        [
            lax.dynamic_update_slice(
                jnp.zeros((KW, DIN), jnp.float32), xk_grad, (0, group * width_dev)
            ),
            bck_grad,
        ],
        axis=1,
    )
    conv_b_grad = jnp.concatenate(
        [
            lax.dynamic_update_slice(jnp.zeros((DIN,), jnp.float32), xo_grad, (group * width_dev,)),
            bco_grad,
        ],
        axis=0,
    )
    head_grads = tuple(
        (
            lax.dynamic_update_slice(
                jnp.zeros((HEADS,), jnp.float32), grad_piece, (group * heads_dev,)
            )
            for grad_piece in (bias_grad, rate_grad, skip_grad)
        )
    )
    lower_grads = (norm_grad, in_weight_grad, conv_w_grad, conv_b_grad)
    return (upstream + stream_grad, lower_grads, head_grads)


def shards(
    inputs, out_grad, norm_gain, w_in, conv_w, conv_b, dt_bias, a_log, d_skip, gnorm_gain, w_out
):
    gathered = (
        lax.all_gather(norm_gain, ("dp", "seq"), axis=1, tiled=True),
        lax.all_gather(w_in, ("dp", "seq"), axis=1, tiled=True),
        lax.all_gather(conv_w, ("dp", "seq"), axis=2, tiled=True),
        lax.all_gather(conv_b, ("dp", "seq"), axis=1, tiled=True),
        lax.all_gather(gnorm_gain, ("dp", "seq"), axis=1, tiled=True),
        lax.all_gather(w_out, ("dp", "seq"), axis=1, tiled=True),
    )
    weights = tuple((tensor[0] for tensor in gathered))
    group = lax.axis_index("seq")
    heads_dev = HEADS // lax.axis_size("seq")
    mix_params = local_params(weights, (dt_bias[0], a_log[0], d_skip[0]), group, heads_dev)
    first_section = lax.axis_index("section") == 0
    micro_count = inputs.shape[0]
    tok_rows = inputs.shape[2]
    features = inputs.shape[3]
    empty = jnp.zeros((tok_rows, features), jnp.float32)
    received = empty
    stash = []
    results = []
    for moment in range(micro_count + 1):
        fresh = inputs[moment, 0].astype(jnp.float32) if moment < micro_count else empty
        current = jnp.where(first_section, fresh, received)
        kept, result = forward_layer(current, weights, mix_params)
        stash.append(kept)
        if moment >= 1:
            results.append(result.astype(jnp.bfloat16))
        if moment < micro_count:
            received = passed_along(result.astype(jnp.bfloat16), "section", 1).astype(result.dtype)
    received = empty
    sums = None
    head_totals = None
    input_grads = [empty] * micro_count
    for moment in range(micro_count + 1):
        if moment < micro_count:
            upstream = out_grad[micro_count - 1 - moment, 0].astype(jnp.float32)
        else:
            upstream = empty
        incoming = jnp.where(first_section, received, upstream)
        kept = stash[micro_count - moment]
        out_weight_grad, gnorm_grad, mixed_grad, gate_grad = back_top(kept, incoming, weights)
        stream_grad, lower_grads, head_grads = back_bottom(
            kept, incoming, weights, mix_params, group, heads_dev, mixed_grad, gate_grad
        )
        if moment >= 1:
            input_grads[micro_count - moment] = stream_grad
        if moment < micro_count:
            received = passed_along(stream_grad.astype(jnp.bfloat16), "section", -1).astype(
                stream_grad.dtype
            )
        big_grads = lower_grads + (gnorm_grad, out_weight_grad)
        head_totals = (
            head_grads
            if head_totals is None
            else tuple((left + right for left, right in zip(head_totals, head_grads)))
        )
        sums = (
            big_grads
            if sums is None
            else tuple((left + right for left, right in zip(sums, big_grads)))
        )
    sums = (
        lax.psum_scatter(sums[0], ("dp", "seq"), scatter_dimension=0, tiled=True),
        lax.psum_scatter(sums[1], ("dp", "seq"), scatter_dimension=0, tiled=True),
        lax.psum_scatter(sums[2], ("dp", "seq"), scatter_dimension=1, tiled=True),
        lax.psum_scatter(sums[3], ("dp", "seq"), scatter_dimension=0, tiled=True),
        lax.psum_scatter(sums[4], ("dp", "seq"), scatter_dimension=0, tiled=True),
        lax.psum_scatter(sums[5], ("dp", "seq"), scatter_dimension=0, tiled=True),
    )
    head_totals = lax.psum(head_totals, ("dp", "seq"))
    out_full = jnp.stack(results)
    grad_full = jnp.stack(input_grads)
    half = features // 2
    payload = jnp.where(
        first_section, grad_full[:, :, half:], out_full[:, :, :half].astype(jnp.float32)
    )
    arrived = from_partner(payload.astype(jnp.bfloat16), "section", 0).astype(payload.dtype)
    out_part = jnp.where(first_section, arrived, out_full[:, :, half:].astype(jnp.float32)).astype(
        jnp.bfloat16
    )
    grad_part = jnp.where(first_section, grad_full[:, :, :half], arrived)
    return (
        out_part[:, None],
        grad_part[:, None],
        sums[0][None],
        sums[1][None],
        sums[2][None],
        sums[3][None],
        head_totals[0][None],
        head_totals[1][None],
        head_totals[2][None],
        sums[4][None],
        sums[5][None],
    )


def solution(mesh):
    in_specs = (
        P(None, "dp", "seq", None),
        P(None, "dp", "seq", None),
        P("section", ("dp", "seq")),
        P("section", ("dp", "seq"), None),
        P("section", None, ("dp", "seq")),
        P("section", ("dp", "seq")),
        P("section", None),
        P("section", None),
        P("section", None),
        P("section", ("dp", "seq")),
        P("section", ("dp", "seq"), None),
    )
    out_specs = (
        P(None, "dp", "seq", "section"),
        P(None, "dp", "seq", "section"),
        P("section", ("dp", "seq")),
        P("section", ("dp", "seq"), None),
        P("section", None, ("dp", "seq")),
        P("section", ("dp", "seq")),
        P("section", None),
        P("section", None),
        P("section", None),
        P("section", ("dp", "seq")),
        P("section", ("dp", "seq"), None),
    )
    return jax.shard_map(shards, mesh=mesh, in_specs=in_specs, out_specs=out_specs, check_vma=False)
```

profile of v0, /device:TPU:0, one launch (start us, length us, event | category | flops | bytes accessed | tf_op | source)
XLA Modules:
  0.0 2470.5 jit_solution(16843417519295938459)
XLA Ops:
  13.8 351.0 %all-reduce.74 = (bf16[2304]{0:T(1024)(128)(2,1)S(1)}, bf16[1024]{0:T(1024)(128)(2,1)S(1)}, bf16[2048]{0:T(1024)(128)(2,1)}) all-reduce(bf16[2304]{0:T(1024)(128)(2,1)S(1)} %dynamic-update-slice.6, bf16[1024]{0:T(1024)(128)(2,1)S(1)} %dynamic-update-slice.7, ...), channel_id=1, replica_groups=mesh['dp'=4,'section'=2,'seq'=16] {'dp','seq'}, use_global_device_ids=true, to_apply=%add.66 | all-reduce | flops 5376 | bytes 21504
  366.0 7.4 fusion.24
  376.3 176.5 %all_gather.28 = bf16[1,4,2304]{1,0,2:T(2,128)(2,1)S(1)} all-gather(bf16[1,4,36]{1,0,2:T(2,128)(2,1)S(1)} %copy.1225), channel_id=1, replica_groups=mesh['dp'=4,'section'=2,'seq'=16] {'dp','seq'}, dimensions={2}, use_global_device_ids=true | all-gather | bytes 18720 | tf_op jit(solution)/shard_map/all_gather | solution.py:242
  605.4 19.5 while.141
  630.4 6.1 fusion.171
  647.3 10.0 all-to-all-done.2
  666.3 7.3 fusion.27
  679.5 6.3 all-to-all-done.4
  694.0 6.8 all-to-all-done.3
  705.7 8.8 all-gather.12.cloned.1.call-done
  728.0 42.8 %while.142 = (s32[]{:T(128)}, f32[2,128,64]{2,1,0:T(8,128)}, f32[8,2,128,64]{2,3,1,0:T(8,128)}, f32[8,2]{1,0:T(8,128)}, f32[8,2,128,64]{2,3,1,0:T(8,128)}, /*index=5*/s32[]{:T(128)}, s32[]{:T(128)}) while((s32[]{:T(128)}, f32[2,128,64]{2,1,0:T(8,128)}, f32[8,2,128,64]{2,3,1,0:T(8,128)}, f32[8,2]{1,0:T(8,128)}, ...), condition=%wide.region_10.11_spmd.clone, body=%wide.region_9.10_spmd.clone.sunk | while | flops 49155 | bytes 787063 | solution.py:66
  783.0 6.1 fusion.168
  796.3 14.9 all_to_all.252
  821.1 7.3 fusion.30
  864.1 18.1 all-gather.14.cloned.1.call-done
  895.7 31.2 %while.143 = (s32[]{:T(128)}, f32[2,128,64]{2,1,0:T(8,128)}, f32[8,2,128,64]{2,3,1,0:T(8,128)}, f32[8,2]{1,0:T(8,128)}, f32[8,2,128,64]{2,3,1,0:T(8,128)}, /*index=5*/s32[]{:T(128)}, s32[]{:T(128)}) while((s32[]{:T(128)}, f32[2,128,64]{2,1,0:T(8,128)}, f32[8,2,128,64]{2,3,1,0:T(8,128)}, f32[8,2]{1,0:T(8,128)}, ...), condition=%wide.region_16.17_spmd.clone, body=%wide.region_15.16_spmd.clone.sunk | while | flops 49155 | bytes 787063 | solution.py:66
  961.9 6.4 all-to-all-done.8
  987.8 30.4 %while.144 = (s32[]{:T(128)}, f32[2,128,64]{2,1,0:T(8,128)}, f32[8,2,128,64]{3,2,1,0:T(8,128)}, f32[8,2,1,1]{1,3,2,0:T(1,128)}, f32[8,2]{1,0:T(8,128)S(1)}, /*index=5*/f32[8,2,128,64]{2,3,1,0:T(8,128)}, s32[]{:T(128)}, s32[]{:T(128)}) while((s32[]{:T(128)}, f32[2,128,64]{2,1,0:T(8,128)}, f32[8,2,128,64]{3,2,1,0:T(8,128)}, ...), condition=%wide.region_22.24_spmd.clone, body=%wide.region_21.23_spmd.clone.sunk | while | flops 65539 | bytes 788104 | solution.py:66
  1027.2 6.0 convolution_bitcast_fusion.5
  1037.1 45.1 %while.145 = (s32[]{:T(128)}, f32[2,128,64]{2,1,0:T(8,128)S(1)}, f32[8,2]{1,0:T(8,128)}, f32[8,2,128,64]{3,2,1,0:T(8,128)}, f32[8,2,128,64]{2,3,1,0:T(8,128)}, /...) while((s32[]{:T(128)}, f32[2,128,64]{2,1,0:T(8,128)S(1)}, ...), condition=%wide.region_25.27_spmd.clone, body=%wide.region_23.26_spmd.clone.sunk | while | flops 98306 | bytes 852160 | solution.py:66
  1090.9 6.8 fusion.85
  1116.7 6.6 convolution_add_fusion.4
  1125.8 6.6 multiply_reduce_fusion.13
  1144.5 7.5 all-to-all-start.10
  1166.2 7.3 all-to-all-start.11
  1177.0 37.3 %reduce-scatter.17.cloned.1.call-done = bf16[128,256]{1,0:T(8,128)(2,1)} async-done(((bf16[2048,256]{1,0:T(8,128)(2,1)}), bf16[128,256]{1,0:T(8,128)(2,1)}) %reduce-scatter.17.cloned.1.call-update) | async-done | bytes 65552
  1215.4 7.8 multiply_reduce_fusion.41
  1240.8 29.5 %while.146 = (s32[]{:T(128)}, f32[2,128,64]{2,1,0:T(8,128)S(1)}, f32[8,2,128,64]{3,2,1,0:T(8,128)}, f32[8,2,1,1]{1,3,2,0:T(1,128)}, f32[8,2]{1,0:T(8,128)}, /*index=5*/f32[8,2,128,64]{2,3,1,0:T(8,128)}, s32[]{:T(128)}, s32[]{:T(128)}) while((s32[]{:T(128)}, f32[2,128,64]{2,1,0:T(8,128)S(1)}, f32[8,2,128,64]{3,2,1,0:T(8,128)}, ...), condition=%wide.region_41.43_spmd.clone, body=%wide.region_40.42_spmd.clone.sunk | while | flops 65539 | bytes 788608 | solution.py:66
  1292.1 45.6 %while.147 = (s32[]{:T(128)}, f32[2,128,64]{2,1,0:T(8,128)S(1)}, f32[8,2]{1,0:T(8,128)}, f32[8,2,128,64]{3,2,1,0:T(8,128)}, f32[8,2,128,64]{2,3,1,0:T(8,128)}, /...) while((s32[]{:T(128)}, f32[2,128,64]{2,1,0:T(8,128)S(1)}, ...), condition=%wide.region_44.46_spmd.clone, body=%wide.region_42.45_spmd.clone.sunk | while | flops 98306 | bytes 852160 | solution.py:66
  1346.4 6.7 fusion.87
  1372.3 6.3 convolution_add_fusion.2
  1381.2 6.6 multiply_reduce_fusion.9
  1399.8 7.8 all-to-all-start.13
  1420.5 7.3 all-to-all-start.14
  1432.7 38.3 %reduce-scatter.19.cloned.1.call-done = bf16[128,256]{1,0:T(8,128)(2,1)} async-done(((bf16[2048,256]{1,0:T(8,128)(2,1)}), bf16[128,256]{1,0:T(8,128)(2,1)}) %reduce-scatter.19.cloned.1.call-update) | async-done | bytes 65552
  1472.0 7.8 multiply_reduce_fusion.40
  1498.5 29.0 %while.148 = (s32[]{:T(128)}, f32[2,128,64]{2,1,0:T(8,128)S(1)}, f32[8,2,128,64]{3,2,1,0:T(8,128)}, f32[8,2,1,1]{1,3,2,0:T(1,128)}, f32[8,2]{1,0:T(8,128)}, /*index=5*/f32[8,2,128,64]{2,3,1,0:T(8,128)}, s32[]{:T(128)}, s32[]{:T(128)}) while((s32[]{:T(128)}, f32[2,128,64]{2,1,0:T(8,128)S(1)}, f32[8,2,128,64]{3,2,1,0:T(8,128)}, ...), condition=%wide.region_60.62_spmd.clone, body=%wide.region_59.61_spmd.clone.sunk | while | flops 65539 | bytes 788608 | solution.py:66
  1544.8 44.8 %while.149 = (s32[]{:T(128)}, f32[2,128,64]{2,1,0:T(8,128)S(1)}, f32[8,2]{1,0:T(8,128)}, f32[8,2,128,64]{3,2,1,0:T(8,128)}, f32[8,2,128,64]{2,3,1,0:T(8,128)}, /...) while((s32[]{:T(128)}, f32[2,128,64]{2,1,0:T(8,128)S(1)}, ...), condition=%wide.region_63.65_spmd.clone, body=%wide.region_61.64_spmd.clone.sunk | while | flops 98306 | bytes 852160 | solution.py:66
  1589.6 7.0 fusion.89
  1612.5 6.6 multiply_reduce_fusion.5
  1635.4 9.2 fusion.334
  1661.6 7.5 all-to-all-start.16
  1682.6 7.3 all-to-all-start.17
  1690.0 9.1 fusion.333
  1703.5 19.8 add_add_fusion
  1736.0 7.0 multiply_reduce_fusion.39
  1743.7 347.4 %all-reduce.73 = (f32[1024]{0:T(1024)S(1)}, f32[4,2304]{1,0:T(4,128)S(1)}, f32[2304]{0:T(1024)S(1)}, f32[1,32]{1,0:T(1,128)}, f32[1,32]{1,0:T(1,128)}, /*index=5*/f32[1,32]{1,0:T(1,128)}, f32[2048]{0:T(1024)S(1)}) all-reduce(f32[1024]{0:T(1024)S(1)} %add_add_fusion.9, ...), channel_id=5, replica_groups=mesh['dp'=4,'section'=2,'seq'=16] {'dp','seq'}, use_global_device_ids=true, to_apply=%region_78.80.clone | all-reduce | flops 14688 | bytes 117504
  2094.5 368.9 %reduce-scatter.13.cloned.1.call-done = f32[16,4384]{1,0:T(8,128)} async-done(((f32[1024,4384]{1,0:T(8,128)}), f32[16,4384]{1,0:T(8,128)}) %reduce-scatter.13.cloned.1.call-update) | async-done | bytes 280592 | tf_op jit(solution)/shard_map/reduce_scatter | solution.py:302
  (1590 shorter events, 855.4 us)
Async XLA Ops:
  7.2 368.9 %copy-start = (f32[1,32]{1,0:T(1,128)S(1)}, f32[1,32]{1,0:T(1,128)}, u32[]{:S(2)}) copy-start(f32[1,32]{1,0:T(1,128)} %param.36) | copy-start | bytes 388
  7.2 358.8 %all-gather.6.cloned.1.call-start = ((), (), s32[]{:S(2)}) async-start(), calls=%async_computation.23 | async-start | bytes 9318400 | tf_op jit(solution)/shard_map/all_gather | solution.py:241
  7.9 578.2 %all-gather.8.cloned.1.call-start = ((), (), s32[]{:S(2)}) async-start(), calls=%async_computation.24 | async-start | bytes 1114112 | tf_op jit(solution)/shard_map/all_gather | solution.py:137
  373.4 189.2 %copy-start.71 = (bf16[128,4384]{0,1:T(8,128)(2,1)}, bf16[128,4384]{0,1:T(8,128)(2,1)S(1)}, u32[]{:S(2)}) copy-start(bf16[128,4384]{0,1:T(8,128)(2,1)S(1)} %fusion.24) | copy-start | bytes 3366916
  374.1 285.5 %all-gather.10.cloned.1.call-start = ((), (), s32[]{:S(2)}) async-start(), calls=%async_computation.25 | async-start | bytes 4259840 | tf_op jit(solution)/shard_map/all_gather | solution.py:245
  374.9 179.6 %copy-start.313 = (f32[1,32]{1,0:T(1,128)S(1)}, f32[1,32]{1,0:T(1,128)}, u32[]{:S(2)}) copy-start(f32[1,32]{1,0:T(1,128)} %param.38) | copy-start | bytes 388
  376.1 195.4 %copy-start.214 = (f32[2]{0:T(128)}, f32[2]{0:T(128)S(1)}, u32[]{:S(2)}) copy-start(f32[2]{0:T(128)S(1)} %get-tuple-element.1506) | copy-start | bytes 28
  376.2 195.3 %copy-start.210 = (f32[2]{0:T(128)}, f32[2]{0:T(128)S(1)}, u32[]{:S(2)}) copy-start(f32[2]{0:T(128)S(1)} %fusion.405) | copy-start | bytes 28
  554.5 161.5 %copy-start.148 = (f32[256]{0:T(256)}, f32[256]{0:T(256)S(1)}, u32[]{:S(2)}) copy-start(f32[256]{0:T(256)S(1)} %get-tuple-element.1336) | copy-start | bytes 3076
  555.2 11.2 all-to-all-start.1
  566.3 15.2 all-to-all-start
  643.7 13.6 all-to-all-start.2
  647.2 67.2 %all-gather.12.cloned.1.call-start = ((), (), s32[]{:S(2)}) async-start(), calls=%async_computation.26 | async-start | bytes 1114112 | tf_op jit(solution)/shard_map/all_gather | solution.py:137
  663.6 2.4 collective-permute-start
  666.1 148.3 %copy-start.64 = (bf16[128,1024]{1,0:T(8,128)(2,1)}, bf16[128,1024]{1,0:T(8,128)(2,1)S(1)}, u32[]{:S(2)}) copy-start(bf16[128,1024]{1,0:T(8,128)(2,1)S(1)} %collective-permute-done) | copy-start | bytes 786436
  674.9 10.9 all-to-all-start.4
  685.8 15.0 all-to-all-start.3
  703.8 92.4 %copy-start.25 = (f32[2048,128]{1,0:T(8,128)}, f32[2048,128]{1,0:T(8,128)S(1)}, u32[]{:S(2)}) copy-start(f32[2048,128]{1,0:T(8,128)S(1)} %get-tuple-element.1492) | copy-start | bytes 3145732
  704.5 77.1 %copy-start.12 = (f32[16,8,8,256]{3,2,1,0:T(8,128)}, f32[16,8,8,256]{3,2,1,0:T(8,128)S(1)}, u32[]{:S(2)}) copy-start(f32[16,8,8,256]{3,2,1,0:T(8,128)S(1)} %copy.1746) | copy-start | bytes 3145732
  817.9 2.4 collective-permute-start.1
  829.4 11.0 all-to-all-start.7
  832.9 49.4 %all-gather.14.cloned.1.call-start = ((), (), s32[]{:S(2)}) async-start(), calls=%async_computation.27 | async-start | bytes 1114112 | tf_op jit(solution)/shard_map/all_gather | solution.py:137
  840.5 15.2 all-to-all-start.6
  844.9 113.3 %copy-start.114 = (f32[2048,2]{0,1:T(2,128)}, f32[2048,2]{0,1:T(2,128)S(1)}, u32[]{:S(2)}) copy-start(f32[2048,2]{0,1:T(2,128)S(1)} %get-tuple-element.1585) | copy-start | bytes 49156
  846.2 112.0 %copy-start.112 = (f32[8,2,2,128]{3,0,1,2:T(8,128)}, f32[8,2,2,128]{3,0,1,2:T(8,128)S(1)}, u32[]{:S(2)}) copy-start(f32[8,2,2,128]{3,0,1,2:T(8,128)S(1)} %reduce-window.70) | copy-start | bytes 49156
  952.9 15.4 all-to-all-start.8
  981.8 38.7 %all-to-all-start.9 = ((bf16[128,16,128]{2,0,1:T(8,128)(2,1)}), bf16[128,16,128]{2,0,1:T(8,128)(2,1)}, u32[]{:S(2)}, u32[]{:S(2)}) async-start(bf16[128,16,128]{2,0,1:T(8,128)(2,1)} %copy.1296), calls=%async_computation.9 | async-start | bytes 1048576 | tf_op jit(solution)/shard_map/all_to_all | solution.py:169
  986.1 228.2 %reduce-scatter.17.cloned.1.call-start = ((), (), s32[]{:S(2)}) async-start(), calls=%async_computation.30 | async-start | bytes 1114112
  1144.5 21.8 all-to-all-start.10
  1152.2 63.2 %copy-start.68 = (bf16[128,1024]{1,0:T(8,128)(2,1)S(1)}, bf16[128,1024]{1,0:T(8,128)(2,1)}, u32[]{:S(2)}) copy-start(bf16[128,1024]{1,0:T(8,128)(2,1)} %copy-done.67) | copy-start | bytes 786436
  1164.4 58.8 %copy-start.105 = (f32[8,2,2,128]{3,0,1,2:T(8,128)}, f32[8,2,2,128]{3,0,1,2:T(8,128)S(1)}, u32[]{:S(2)}) copy-start(f32[8,2,2,128]{3,0,1,2:T(8,128)S(1)} %reduce-window.76) | copy-start | bytes 49156
  1164.6 58.6 %copy-start.137 = (f32[8,2,2]{0,1,2:T(2,128)}, f32[8,2,2]{0,1,2:T(2,128)S(1)}, u32[]{:S(2)}) copy-start(f32[8,2,2]{0,1,2:T(2,128)S(1)} %copy.1351) | copy-start | bytes 388
  1166.2 49.1 %all-to-all-start.11 = ((bf16[16,128,2]{1,2,0:T(2,128)(2,1)}), bf16[16,128,2]{1,2,0:T(2,128)(2,1)S(1)}, u32[]{:S(2)}, u32[]{:S(2)}) async-start(bf16[16,128,2]{1,2,0:T(2,128)(2,1)} %bitcast.1030), calls=%async_computation.11 | async-start | bytes 16384 | tf_op jit(solution)/shard_map/all_to_all | solution.py:193
  1223.5 3.5 collective-permute-start.2
  1234.1 41.4 %all-to-all-start.12 = ((bf16[128,16,128]{2,0,1:T(8,128)(2,1)}), bf16[128,16,128]{2,0,1:T(8,128)(2,1)}, u32[]{:S(2)}, u32[]{:S(2)}) async-start(bf16[128,16,128]{2,0,1:T(8,128)(2,1)} %copy.1348), calls=%async_computation.12 | async-start | bytes 1048576 | tf_op jit(solution)/shard_map/all_to_all | solution.py:169
  1239.1 231.8 %reduce-scatter.19.cloned.1.call-start = ((), (), s32[]{:S(2)}) async-start(), calls=%async_computation.31 | async-start | bytes 1114112
  1399.8 20.7 all-to-all-start.13
  1407.6 64.3 %copy-start.65 = (bf16[128,1024]{1,0:T(8,128)(2,1)S(1)}, bf16[128,1024]{1,0:T(8,128)(2,1)}, u32[]{:S(2)}) copy-start(bf16[128,1024]{1,0:T(8,128)(2,1)} %copy-done.64) | copy-start | bytes 786436
  1420.5 51.3 %all-to-all-start.14 = ((bf16[16,128,2]{1,2,0:T(2,128)(2,1)}), bf16[16,128,2]{1,2,0:T(2,128)(2,1)S(1)}, u32[]{:S(2)}, u32[]{:S(2)}) async-start(bf16[16,128,2]{1,2,0:T(2,128)(2,1)} %bitcast.1029), calls=%async_computation.14 | async-start | bytes 16384 | tf_op jit(solution)/shard_map/all_to_all | solution.py:193
  1481.0 3.7 collective-permute-start.3
  1491.7 36.4 %all-to-all-start.15 = ((bf16[128,16,128]{2,0,1:T(8,128)(2,1)}), bf16[128,16,128]{2,0,1:T(8,128)(2,1)}, u32[]{:S(2)}, u32[]{:S(2)}) async-start(bf16[128,16,128]{2,0,1:T(8,128)(2,1)} %copy.1400), calls=%async_computation.15 | async-start | bytes 1048576 | tf_op jit(solution)/shard_map/all_to_all | solution.py:169
  1496.7 205.9 %reduce-scatter.21.cloned.1.call-start = ((), (), s32[]{:S(2)}) async-start(), calls=%async_computation.32 | async-start | bytes 1114112
  1624.7 469.9 %reduce-scatter.15.cloned.1.call-start = ((), (), s32[]{:S(2)}) async-start(), calls=%async_computation.29 | async-start | bytes 8519680 | tf_op jit(solution)/shard_map/reduce_scatter | solution.py:306
  1661.6 20.9 all-to-all-start.16
  1682.6 21.0 all-to-all-start.17
  1689.9 773.5 %reduce-scatter.13.cloned.1.call-start = ((), (), s32[]{:S(2)}) async-start(), calls=%async_computation.28 | async-start | bytes 18636800 | tf_op jit(solution)/shard_map/reduce_scatter | solution.py:302
  1743.3 720.2 %copy-start.1 = (f32[1,32]{1,0:T(1,128)S(1)}, f32[1,32]{1,0:T(1,128)}, u32[]{:S(2)}) copy-start(f32[1,32]{1,0:T(1,128)} %param.36) | copy-start | bytes 388
  1743.4 350.2 %collective-permute-start.4 = (bf16[2,128,512]{2,1,0:T(8,128)(2,1)S(1)}, bf16[2,128,512]{2,1,0:T(8,128)(2,1)S(1)}, u32[]{:S(2)}, u32[]{:S(2)}) collective-permute-start(bf16[2,128,512]{2,1,0:T(8,128)(2,1)S(1)} %fusion.285), channel_id=1, source_target_pairs={{0,16},{16,0},{1,17},{17,1},{2,18},{18,2},{3,19},{19,3},{4,20},{20... | collective-permute-start | bytes 786440 | tf_op jit(solution)/shard_map/ppermute | solution.py:25
  (298 other events, 2739.4 us)
Sparse Core Ops, SparseCore 0:
  10.9 83.9 all-gather.5
  374.2 36.5 all-gather.7
  413.7 71.0 all-gather.9
  674.4 40.0 all-gather.11
  836.8 45.4 all-gather.13
  1138.2 76.1 reduce-scatter.16
  1393.5 77.3 reduce-scatter.18
  1624.8 77.7 reduce-scatter.20
  1705.7 368.1 reduce-scatter.14
  2076.8 386.5 reduce-scatter.12
where the time goes:
time: 2490 us; the launch traced here: 2470 us
  blocking collectives  890 us (36%)
  waiting for transfers between devices  523 us (21%)
  local copies, waits for them, and re-layouts  421 us (17%)
  matrix products  276 us (11%)
  other arithmetic  240 us (10%)
  starting transfers between devices  96.6 us (4%)
    unnamed x2, blocking collectives  698 us
    reduce_scatter x1, waiting for transfers between devices, shards(): lax.psum_scatter(sums[1], ('dp', 'seq'), scatter_dimension=0, tiled=True)  369 us
    all_gather x1, blocking collectives, shards(): lax.all_gather(conv_w, ('dp', 'seq'), axis=2, tiled=True)  177 us
    dynamic_slice x144, local copies, waits for them, and re-layouts, state_space(): _, entering = lax.scan(carry_step, initial, (totals, block_states))  79.4 us
    unnamed x13, waiting for transfers between devices  79.2 us
    dynamic_update_slice x96, local copies, waits for them, and re-layouts, state_space(): _, entering = lax.scan(carry_step, initial, (totals, block_states))  71.9 us
    mul x72, local copies, waits for them, and re-layouts, carry_step(): return (factor[:, None, None] * carried + added, carried)  54.8 us
  transfers between devices with their start and end apart: 32, of which 16 were waited for; matrix products, arithmetic and copies ran while one was open for 15% of the time, Pallas kernels for 0%

commit v1 on v0

v1 whole, which is shorter than its diff:
```python
import jax
import jax.numpy as jnp
from jax import lax
from jax.experimental import pallas as pl
from jax.experimental.pallas import tpu as pltpu
from jax.sharding import PartitionSpec as P

DIN = 2048
HEADS = 32
STATE = 128
KW = 4
EIN = 4384
EINP = 4480
CONV_CH = 2304
DT_COL = 2 * DIN + 2 * STATE
T = 128
PAIRS = 16
PAY = STATE + 16

f32 = jnp.float32
bf16 = jnp.bfloat16
epsilon = 1e-05
highest = lax.Precision.HIGHEST
both = ("dp", "seq")


def dot(a, b, precision=None):
    return jnp.dot(a, b, preferred_element_type=f32, precision=precision)


def dot_nt(a, b):
    return lax.dot_general(a, b, (((1,), (1,)), ((), ())), preferred_element_type=f32)


def dot_tn(a, b):
    return lax.dot_general(a, b, (((0,), (0,)), ((), ())), preferred_element_type=f32)


def low_half():
    return lax.broadcasted_iota(jnp.int32, (1, T), 1) < 64


def lower_triangle():
    rows = lax.broadcasted_iota(jnp.int32, (T, T), 0)
    columns = lax.broadcasted_iota(jnp.int32, (T, T), 1)
    return rows >= columns


def sigmoid(v):
    return 1.0 / (1.0 + jnp.exp(-v))


def silu_and_slope(v):
    s = sigmoid(v)
    return v * s, s * (1.0 + v * (1.0 - s))


def spread(table, j):
    return jnp.where(low_half(), table[:, 2 * j : 2 * j + 1], table[:, 2 * j + 1 : 2 * j + 2])


def block(j):
    return slice(j * T, (j + 1) * T)


def conv_block(padded, taps, j):
    total = taps[KW : KW + 1, block(j)] + taps[0:1, block(j)] * padded[13 : 13 + T, block(j)]
    for k in range(1, KW):
        total = total + taps[k : k + 1, block(j)] * padded[13 + k : 13 + k + T, block(j)]
    return total


def load_padded(padded, projected, halo):
    padded[0:16, :] = halo[...].astype(f32)
    padded[16 : 16 + T, :] = projected[:, DIN:DT_COL].astype(f32)


def put_payload(payload, j, state, totals):
    payload[j, 0:STATE, :] = state.astype(bf16)
    factor = spread(totals, j)
    high = factor.astype(bf16).astype(f32)
    rest = factor - high
    row = lax.broadcasted_iota(jnp.int32, (16, T), 0)
    extra = jnp.where(row == 0, high, jnp.where(row == 1, rest, 0.0))
    payload[j, STATE:PAY, :] = extra.astype(bf16)


def front_kernel(projected, halo, taps, heads, xs, bc, delta, cum, payload, padded):
    load_padded(padded, projected, halo)
    lane = lax.broadcasted_iota(jnp.int32, (1, T), 1)
    raw = projected[:, DT_COL:EINP].astype(f32) + heads[0:1, :]
    soft = jnp.maximum(raw, 0.0) + jnp.log1p(jnp.exp(-jnp.abs(raw)))
    steps = jnp.where(lane < HEADS, soft, 0.0)
    delta[...] = steps
    logs = steps * -jnp.exp(heads[1:2, :])
    sums = dot(lower_triangle().astype(f32), logs, highest)
    cum[...] = sums
    last = sums[T - 1 : T, :]
    weight = jnp.exp(last - sums) * steps
    totals = jnp.exp(last)
    b_pre = conv_block(padded, taps, PAIRS)
    c_pre = conv_block(padded, taps, PAIRS + 1)
    keys = b_pre * sigmoid(b_pre)
    bc[:, 0:STATE] = keys.astype(bf16)
    bc[:, STATE:] = (c_pre * sigmoid(c_pre)).astype(bf16)
    keys_t = keys.T.astype(bf16)
    for j in range(PAIRS):
        pre = conv_block(padded, taps, j)
        x = pre * sigmoid(pre)
        xs[:, block(j)] = x
        put_payload(payload, j, dot(keys_t, (spread(weight, j) * x).astype(bf16)), totals)


def scan_kernel(backward, payload, entering):
    carried = jnp.zeros((STATE, T), f32)
    order = range(PAIRS - 1, -1, -1) if backward else range(PAIRS)
    for k in order:
        entering[k] = carried.astype(bf16)
        extra = payload[k, STATE:PAY, :].astype(f32)
        factor = extra[0:1, :] + extra[1:2, :]
        carried = factor * carried + payload[k, 0:STATE, :].astype(f32)


def decay(cum, cum_t, h, causal):
    return jnp.where(causal, jnp.exp(cum[:, h : h + 1] - cum_t[h : h + 1, :]), 0.0)


def halves(v):
    return jnp.concatenate(
        [jnp.where(low_half(), v, 0.0), jnp.where(low_half(), 0.0, v)], axis=0
    ).astype(bf16)


def within_kernel(xs, bc, delta, cum, heads, local):
    causal = lower_triangle()
    cums = cum[...]
    cum_t = cums.T
    steps = delta[...]
    skips = heads[2:3, :]
    scores = dot_nt(bc[:, STATE:], bc[:, 0:STATE])
    for j in range(PAIRS):
        x = xs[:, block(j)]
        mixing = jnp.concatenate(
            [scores * decay(cums, cum_t, 2 * j + i, causal) for i in range(2)], axis=1
        ).astype(bf16)
        local[:, block(j)] = dot(mixing, halves(spread(steps, j) * x)) + spread(skips, j) * x


def finish_kernel(local, bc, cum, entering, projected, gain, mixed, normed, gated):
    growth = jnp.exp(cum[...])
    queries = bc[:, STATE:]
    squares = jnp.zeros((T, T), f32)
    for j in range(PAIRS):
        whole = local[:, block(j)] + spread(growth, j) * dot(queries, entering[j])
        rounded = whole.astype(bf16)
        mixed[:, block(j)] = rounded
        gate = projected[:, block(j)].astype(f32)
        u = rounded.astype(f32) * (gate * sigmoid(gate))
        gated[:, block(j)] = u
        squares = squares + u * u
    scale = lax.rsqrt(jnp.sum(squares, axis=1, keepdims=True) / DIN + epsilon)
    for j in range(PAIRS):
        normed[:, block(j)] = (gated[:, block(j)] * scale * gain[0:1, block(j)]).astype(bf16)


def top_kernel(
    upstream, mixed, projected, gain, bc, cum, d_mixed, d_gate, d_gain, payload, gated
):
    squares = jnp.zeros((T, T), f32)
    products = jnp.zeros((T, T), f32)
    for j in range(PAIRS):
        gate = projected[:, block(j)].astype(f32)
        u = mixed[:, block(j)].astype(f32) * (gate * sigmoid(gate))
        gated[:, block(j)] = u
        squares = squares + u * u
        products = products + upstream[:, block(j)] * gain[0:1, block(j)] * u
    scale = lax.rsqrt(jnp.sum(squares, axis=1, keepdims=True) / DIN + epsilon)
    pull = scale * scale * scale * (jnp.sum(products, axis=1, keepdims=True) / DIN)
    cums = cum[...]
    growth = jnp.exp(cums)
    totals = growth[T - 1 : T, :]
    queries_t = bc[:, STATE:].astype(f32).T.astype(bf16)
    for j in range(PAIRS):
        gate = projected[:, block(j)].astype(f32)
        act, slope = silu_and_slope(gate)
        u = gated[:, block(j)]
        up = upstream[:, block(j)]
        d_gain[:, block(j)] = jnp.broadcast_to(
            jnp.sum(up * u * scale, axis=0, keepdims=True), (8, T)
        )
        du = up * gain[0:1, block(j)] * scale - u * pull
        dm = (du * act).astype(bf16)
        d_mixed[:, block(j)] = dm
        d_gate[:, block(j)] = (du * mixed[:, block(j)].astype(f32) * slope).astype(bf16)
        put_payload(
            payload, j, dot(queries_t, (spread(growth, j) * dm.astype(f32)).astype(bf16)), totals
        )


def inner_kernel(xs, bc, delta, cum, d_mixed, entering, d_scaled, d_bc, d_cum, rows, columns):
    causal = lower_triangle()
    cums = cum[...]
    cum_t = cums.T
    steps = delta[...]
    growth = jnp.exp(cums)
    keys = bc[:, 0:STATE]
    queries = bc[:, STATE:]
    scores = dot_nt(queries, keys)
    rows[...] = jnp.zeros((T, T), f32)
    columns[...] = jnp.zeros((T, T), f32)
    d_scores = jnp.zeros((T, T), f32)
    d_queries = jnp.zeros((T, STATE), f32)
    for j in range(PAIRS):
        dy_low = d_mixed[:, block(j)]
        dy = dy_low.astype(f32)
        scaled = halves(spread(steps, j) * xs[:, block(j)])
        d_mixing = dot_nt(dy_low, scaled)
        grown = spread(growth, j) * dy
        across = grown * dot(queries, entering[j])
        d_queries = d_queries + dot_nt(grown.astype(bf16), entering[j])
        mixings = []
        for i in range(2):
            h = 2 * j + i
            fall = decay(cums, cum_t, h, causal)
            d_part = d_mixing[:, i * T : (i + 1) * T] * fall
            d_scores = d_scores + d_part
            mixings.append(scores * fall)
            logs = d_part * scores
            own = jnp.where(low_half(), across, 0.0) if i == 0 else jnp.where(low_half(), 0.0, across)
            rows[:, h : h + 1] = jnp.sum(logs + own, axis=1, keepdims=True)
            columns[h : h + 1, :] = jnp.sum(logs, axis=0, keepdims=True)
        d_scaled[:, block(j)] = dot_tn(
            jnp.concatenate(mixings, axis=0).astype(bf16), halves(dy)
        )
    d_low = d_scores.astype(bf16)
    d_bc[:, 0:STATE] = dot_tn(d_low, queries)
    d_bc[:, STATE:] = d_queries + dot(d_low, keys)
    d_cum[...] = rows[...] - columns[...].T


def outer_kernel(
    projected, halo, taps, heads, xs, bc, delta, cum, d_mixed, d_scaled, d_bc, d_cum, entering,
    leaving, d_conv, d_dt, d_taps, d_heads, padded, falls, direct, rest,
):
    load_padded(padded, projected, halo)
    lane = lax.broadcasted_iota(jnp.int32, (1, T), 1)
    cums = cum[...]
    steps = delta[...]
    last = cums[T - 1 : T, :]
    weight = jnp.exp(last - cums)
    totals = jnp.exp(last)
    skips = heads[2:3, :]
    keys = bc[:, 0:STATE]
    falls[...] = jnp.zeros((T, T), f32)
    direct[...] = jnp.zeros((T, T), f32)
    rest[...] = jnp.zeros((8, T), f32)
    low = low_half()

    def conv_back(j, grad):
        pre = conv_block(padded, taps, j)
        d_pre = grad * silu_and_slope(pre)[1]
        d_conv[:, block(j)] = d_pre
        for k in range(KW):
            d_taps[k : k + 1, block(j)] = jnp.sum(
                d_pre * padded[13 + k : 13 + k + T, block(j)], axis=0, keepdims=True
            )
        d_taps[KW : KW + 1, block(j)] = jnp.sum(d_pre, axis=0, keepdims=True)

    d_taps[KW + 1 : 8, :] = jnp.zeros((8 - KW - 1, CONV_CH), f32)
    d_keys = d_bc[:, 0:STATE]
    for j in range(PAIRS):
        x = xs[:, block(j)]
        dy = d_mixed[:, block(j)].astype(f32)
        step = spread(steps, j)
        fall = spread(weight, j)
        weighted = fall * (step * x)
        back = dot(keys, leaving[j])
        d_keys = d_keys + dot_nt(weighted.astype(bf16), leaving[j])
        ds = d_scaled[:, block(j)] + fall * back
        flow = weighted * back
        touch = ds * x
        kept = jnp.sum(leaving[j].astype(f32) * entering[j].astype(f32), axis=0, keepdims=True)
        kept = kept * spread(totals, j)
        skipped = jnp.sum(dy * x, axis=0, keepdims=True)
        for i in range(2):
            h = 2 * j + i
            pick = (lambda v: jnp.where(low, v, 0.0)) if i == 0 else (lambda v: jnp.where(low, 0.0, v))
            falls[:, h : h + 1] = jnp.sum(pick(flow), axis=1, keepdims=True)
            direct[:, h : h + 1] = jnp.sum(pick(touch), axis=1, keepdims=True)
            rest[0:1, h : h + 1] = jnp.sum(pick(kept), axis=1, keepdims=True)
            rest[1:2, h : h + 1] = jnp.sum(pick(skipped), axis=1, keepdims=True)
        conv_back(j, step * ds + spread(skips, j) * dy)
    conv_back(PAIRS, d_keys)
    conv_back(PAIRS + 1, d_bc[:, STATE:])
    flows = falls[...]
    gained = rest[0:1, :] + jnp.sum(flows, axis=0, keepdims=True)
    row = lax.broadcasted_iota(jnp.int32, (T, T), 0)
    d_sums = d_cum[...] - flows + jnp.where(row == T - 1, gained, 0.0)
    upper = lower_triangle().astype(f32).T
    d_logs = dot(upper, d_sums, highest)
    rate = -jnp.exp(heads[1:2, :])
    d_delta = direct[...] + d_logs * rate
    slope = sigmoid(projected[:, DT_COL:EINP].astype(f32) + heads[0:1, :])
    grad = jnp.where(lane < HEADS, d_delta * slope, 0.0)
    d_dt[...] = grad
    d_heads[...] = jnp.zeros((8, T), f32)
    d_heads[0:1, :] = jnp.sum(grad, axis=0, keepdims=True)
    d_heads[1:2, :] = jnp.sum(d_logs * steps, axis=0, keepdims=True) * rate
    d_heads[2:3, :] = rest[1:2, :]


def bottom_kernel(d_conv, halo, taps, d_gate, d_dt, d_projected, padded):
    padded[0:T, :] = d_conv[...]
    padded[T : T + 8, :] = halo[...]
    d_projected[:, 0:DIN] = d_gate[...]
    for j in range(CONV_CH // T):
        total = taps[KW - 1 : KW, block(j)] * padded[0:T, block(j)]
        for k in range(KW - 1):
            shift = KW - 1 - k
            total = total + taps[k : k + 1, block(j)] * padded[shift : shift + T, block(j)]
        d_projected[:, DIN + j * T : DIN + (j + 1) * T] = total.astype(bf16)
    d_projected[:, DT_COL:EINP] = d_dt[...].astype(bf16)


def call(kernel, outs, scratch, name, *args):
    return pl.pallas_call(
        kernel,
        out_shape=[jax.ShapeDtypeStruct(shape, dtype) for shape, dtype in outs],
        scratch_shapes=[pltpu.VMEM(shape, f32) for shape in scratch],
        compiler_params=pltpu.CompilerParams(vmem_limit_bytes=40 * 2**20),
        name=name,
    )(*args)


def swap(value):
    return lax.ppermute(value, "section", [(0, 1), (1, 0)])


def turned(value, axis, steps):
    if axis == "z":
        return lax.ppermute(value, "dp", [(i, (i + steps) % 4) for i in range(4)])
    pairs = []
    for i in range(16):
        x, y = divmod(i, 4)
        if axis == "x":
            pairs.append((i, (x + steps) % 4 * 4 + y))
        else:
            pairs.append((i, x * 4 + (y + steps) % 4))
    return lax.ppermute(value, "seq", pairs)


def coordinate(axis):
    if axis == "z":
        return lax.axis_index("dp")
    seq = lax.axis_index("seq")
    return seq // 4 if axis == "x" else seq % 4


def summed_over(value, order):
    names = ["z", "x", "y"]
    for axis in order:
        at = names.index(axis)
        names.pop(at)
        me = coordinate(axis)

        def piece(steps):
            return lax.dynamic_index_in_dim(value, (me + steps) % 4, at, keepdims=False)

        total = piece(0).astype(f32)
        for steps in (1, -1, 2):
            total = total + turned(piece(steps), axis, steps).astype(f32)
        value = total.astype(bf16)
    return value


def reduced(grad, rows, cuts):
    columns = grad.shape[1]
    shaped = grad.reshape(64, 2, rows // 2, columns)
    section = lax.axis_index("section")
    mine = lax.dynamic_index_in_dim(shaped, section, 1, keepdims=False)
    theirs = lax.dynamic_index_in_dim(shaped, 1 - section, 1, keepdims=False)
    total = (mine.astype(f32) + swap(theirs).astype(f32)).astype(bf16)
    total = total.reshape(4, 4, 4, rows // 2, columns)
    pieces = []
    for order, (start, stop) in zip(("zxy", "xyz", "yzx"), cuts):
        pieces.append(summed_over(total[..., start:stop], order))
    return jnp.concatenate(pieces, axis=-1)


def own_layer(halves_of, first):
    keep = jnp.where(first, halves_of[0], halves_of[1])
    give = jnp.where(first, halves_of[1], halves_of[0])
    came = swap(give.astype(f32))
    keep = keep.astype(f32)
    return jnp.where(
        first, jnp.concatenate([keep, came], axis=0), jnp.concatenate([came, keep], axis=0)
    )


def exchange(payload, backward):
    moved = lax.all_to_all(payload, "seq", split_axis=0, concat_axis=0, tiled=True)
    (entering,) = call(
        lambda *refs: scan_kernel(backward, *refs),
        [((PAIRS, STATE, T), bf16)],
        [],
        "scan_back" if backward else "scan",
        moved,
    )
    return lax.all_to_all(entering, "seq", split_axis=0, concat_axis=0, tiled=True)


def forward_layer(stream, w):
    inverse = lax.rsqrt(jnp.mean(stream * stream, axis=-1, keepdims=True) + epsilon)
    hidden = (stream * inverse * w["norm"]).astype(bf16)
    projected = dot(hidden, w["w_in"]).astype(bf16)
    halo = lax.ppermute(
        projected[T - 16 :, DIN:DT_COL], "seq", [(i, i + 1) for i in range(15)]
    )
    xs, bc, delta, cum, payload = call(
        front_kernel,
        [((T, DIN), f32), ((T, 2 * STATE), bf16), ((T, T), f32), ((T, T), f32), ((PAIRS, PAY, T), bf16)],
        [(T + 16, CONV_CH)],
        "front",
        projected,
        halo,
        w["taps"],
        w["heads"],
    )
    entering = exchange(payload, False)
    (local,) = call(within_kernel, [((T, DIN), f32)], [], "within", xs, bc, delta, cum, w["heads"])
    mixed, normed = call(
        finish_kernel,
        [((T, DIN), bf16), ((T, DIN), bf16)],
        [(T, DIN)],
        "finish",
        local,
        bc,
        cum,
        entering,
        projected,
        w["gnorm"],
    )
    result = stream + dot(normed, w["w_out"])
    return (stream, hidden, projected, halo, xs, bc, delta, cum, entering, mixed, normed), result


def backward_layer(kept, upstream, w):
    stream, hidden, projected, halo, xs, bc, delta, cum, entering, mixed, normed = kept
    upstream_low = upstream.astype(bf16)
    d_normed = dot_nt(upstream_low, w["w_out"])
    grad_out = dot_tn(normed, upstream_low).astype(bf16)
    d_mixed, d_gate, d_gain, payload = call(
        top_kernel,
        [((T, DIN), bf16), ((T, DIN), bf16), ((8, DIN), f32), ((PAIRS, PAY, T), bf16)],
        [(T, DIN)],
        "top",
        d_normed,
        mixed,
        projected,
        w["gnorm"],
        bc,
        cum,
    )
    leaving = exchange(payload, True)
    d_scaled, d_bc, d_cum = call(
        inner_kernel,
        [((T, DIN), f32), ((T, 2 * STATE), f32), ((T, T), f32)],
        [(T, T), (T, T)],
        "inner",
        xs,
        bc,
        delta,
        cum,
        d_mixed,
        entering,
    )
    d_conv, d_dt, d_taps, d_heads = call(
        outer_kernel,
        [((T, CONV_CH), f32), ((T, T), f32), ((8, CONV_CH), f32), ((8, T), f32)],
        [(T + 16, CONV_CH), (T, T), (T, T), (8, T)],
        "outer",
        projected,
        halo,
        w["taps"],
        w["heads"],
        xs,
        bc,
        delta,
        cum,
        d_mixed,
        d_scaled,
        d_bc,
        d_cum,
        entering,
        leaving,
    )
    halo_back = lax.ppermute(d_conv[0:8], "seq", [(i + 1, i) for i in range(15)])
    (d_projected,) = call(
        bottom_kernel,
        [((T, EINP), bf16)],
        [(T + 8, CONV_CH)],
        "bottom",
        d_conv,
        halo_back,
        w["taps"],
        d_gate,
        d_dt,
    )
    grad_in = dot_tn(hidden, d_projected).astype(bf16)
    d_hidden = dot_nt(d_projected, w["w_in"])
    inverse = lax.rsqrt(jnp.mean(stream * stream, axis=-1, keepdims=True) + epsilon)
    grad_norm = jnp.sum(d_hidden * stream * inverse, axis=0)
    scaled = d_hidden * w["norm"]
    pull = inverse * inverse * inverse * jnp.mean(scaled * stream, axis=-1, keepdims=True)
    result = upstream + scaled * inverse - stream * pull
    small = pack_small(grad_norm, d_taps, d_gain[0], d_heads)
    return result, grad_in, grad_out, small


def pack_small(grad_norm, d_taps, d_gain, d_heads):
    def padded(v):
        return jnp.pad(v, ((0, 0), (0, T - v.shape[1])))

    rows = [padded(d_taps[k].reshape(64, 36)) for k in range(KW + 1)]
    rows.append(padded(grad_norm.reshape(64, 16)))
    rows.append(padded(d_gain.reshape(64, 32)))
    heads = d_heads[0:3, 0:HEADS].reshape(1, 3 * HEADS)
    rows.append(jnp.broadcast_to(padded(heads), (64, T)))
    return jnp.stack(rows, axis=1)


def gathered_weights(norm_gain, w_in, conv_w, conv_b, dt_bias, a_log, d_skip, gnorm_gain, w_out):
    def tail(v):
        return jnp.pad(v, ((0, 0), (0, T - v.shape[1])))

    small = jnp.concatenate(
        [tail(conv_w[0]), tail(conv_b), tail(norm_gain), tail(gnorm_gain), jnp.zeros((9, T), bf16)],
        axis=0,
    )
    payload = jnp.concatenate(
        [jnp.pad(w_in[0], ((0, 0), (0, EINP - EIN))), w_out[0, 0:16], w_out[0, 16:32], small], axis=1
    )
    whole = lax.all_gather(payload, ("section", "dp", "seq"), axis=0, tiled=True)
    whole = whole.reshape(2, 64, 16, payload.shape[1])
    heads = jnp.pad(jnp.concatenate([dt_bias, a_log, d_skip], axis=0), ((0, 5), (0, T - HEADS)))
    other = swap(heads)
    first = lax.axis_index("section") == 0
    layers = []
    for l in range(2):
        part = whole[l]
        out = part[:, :, EINP : EINP + 2048].reshape(64, 16, 2, 1024)
        tiny = part[:, :, EINP + 2048 :]
        taps = jnp.stack([tiny[:, k, :36].reshape(CONV_CH) for k in range(KW + 1)]).astype(f32)
        layers.append(
            {
                "w_in": part[:, :, :EINP].reshape(1024, EINP),
                "w_out": jnp.swapaxes(out, 1, 2).reshape(DIN, 1024),
                "taps": jnp.pad(taps, ((0, 8 - KW - 1), (0, 0))),
                "norm": tiny[:, 5, :16].reshape(1, 1024).astype(f32),
                "gnorm": tiny[:, 6, :32].reshape(1, DIN).astype(f32),
                "heads": jnp.where(first == (l == 0), heads, other),
            }
        )
    return layers


def shards(
    inputs, out_grad, norm_gain, w_in, conv_w, conv_b, dt_bias, a_log, d_skip, gnorm_gain, w_out
):
    section = lax.axis_index("section")
    first = section == 0
    layers = gathered_weights(
        norm_gain, w_in, conv_w, conv_b, dt_bias, a_log, d_skip, gnorm_gain, w_out
    )
    stream = lax.dynamic_index_in_dim(inputs, section, 0, keepdims=False)[0].astype(f32)
    g = lax.dynamic_index_in_dim(out_grad, section, 0, keepdims=False)[0].astype(f32)
    kept = []
    for l in range(2):
        saved, stream = forward_layer(stream, layers[l])
        kept.append(saved)
    outputs = stream.astype(bf16)
    in_halves, out_halves, smalls = [None, None], [None, None], [None, None]
    for l in (1, 0):
        g, grad_in, grad_out, smalls[l] = backward_layer(kept[l], g, layers[l])
        out_halves[l] = reduced(grad_out, 32, ((0, 384), (384, 768), (768, 1024)))
        in_halves[l] = reduced(grad_in, 16, ((0, 1536), (1536, 3072), (3072, EINP)))
    grad_w_in = own_layer(in_halves, first)[:, :EIN]
    grad_w_out = own_layer(out_halves, first)
    small = jnp.where(first, smalls[0], smalls[1]) + swap(jnp.where(first, smalls[1], smalls[0]))
    small = jnp.sum(lax.all_to_all(small, both, split_axis=0, concat_axis=0, tiled=True), axis=0)

    half = outputs.shape[1] // 2

    def by_features(value):
        low, high = value[:, :half], value[:, half:]
        came = swap(jnp.where(first, high, low).astype(bf16)).astype(value.dtype)
        keep = jnp.where(first, low, high)
        return jnp.where(first, jnp.stack([keep, came]), jnp.stack([came, keep]))[:, None]

    return (
        by_features(outputs),
        by_features(g),
        small[5:6, :16],
        grad_w_in[None],
        small[None, 0:KW, :36],
        small[KW : KW + 1, :36],
        small[7:8, 0:HEADS],
        small[7:8, HEADS : 2 * HEADS],
        small[7:8, 2 * HEADS : 3 * HEADS],
        small[6:7, :32],
        grad_w_out[None],
    )


def solution(mesh):
    in_specs = (
        P(None, "dp", "seq", None),
        P(None, "dp", "seq", None),
        P("section", both),
        P("section", both, None),
        P("section", None, both),
        P("section", both),
        P("section", None),
        P("section", None),
        P("section", None),
        P("section", both),
        P("section", both, None),
    )
    out_specs = (
        P(None, "dp", "seq", "section"),
        P(None, "dp", "seq", "section"),
        P("section", both),
        P("section", both, None),
        P("section", None, both),
        P("section", both),
        P("section", None),
        P("section", None),
        P("section", None),
        P("section", both),
        P("section", both, None),
    )
    return jax.shard_map(shards, mesh=mesh, in_specs=in_specs, out_specs=out_specs, check_vma=False)
```

time: 2490 us -> 783 us (0.31)
  the two profiles are of different devices: /device:TPU:0 before, /device:TPU:1 now
where the time goes in v1:
time: 783 us; the launch traced here: 774 us
  waiting for transfers between devices  227 us (29%)
  starting transfers between devices  219 us (28%)
  local copies, waits for them, and re-layouts  166 us (21%)
  matrix products  48 us (6%)
  Pallas kernels  45 us (6%)
  other arithmetic  33.4 us (4%)
  blocking collectives  17.9 us (2%)
  between operations  17.1 us (2%)
    all_gather x1, waiting for transfers between devices, gathered_weights(): lax.all_gather(payload, ('section', 'dp', 'seq'), axis=0, tiled=True)  96.6 us
    ppermute x72, waiting for transfers between devices, turned(): return lax.ppermute(value, 'seq', pairs)  78.1 us
    ppermute x72, starting transfers between devices, turned(): return lax.ppermute(value, 'seq', pairs)  74.4 us
    unnamed x272, local copies, waits for them, and re-layouts  58.4 us
    ppermute x10, starting transfers between devices, swap(): return lax.ppermute(value, 'section', [(0, 1), (1, 0)])  51.4 us
    pallas_call x18, Pallas kernels, call(): pl.pallas_call(kernel, out_shape=[jax.ShapeDtypeStruct(shape, dtype) for...  45 us
    ppermute x36, starting transfers between devices, turned(): return lax.ppermute(value, 'dp', [(i, (i + steps) % 4) for i in range(4)])  34.5 us
    ppermute x36, waiting for transfers between devices, turned(): return lax.ppermute(value, 'dp', [(i, (i + steps) % 4) for i in range(4)])  31 us
  transfers between devices with their start and end apart: 131, of which 64 were waited for; matrix products, arithmetic and copies ran while one was open for 19% of the time, Pallas kernels for 5%

profile of v1, /device:TPU:1, one launch (start us, length us, event | category | flops | bytes accessed | tf_op | source)
XLA Modules:
  0.0 774.3 jit_solution(13806975704123070111)
XLA Ops:
  16.5 96.6 %all-gather.2.cloned.1.call-done = bf16[2048,6656]{1,0:T(8,128)(2,1)} async-done(((bf16[16,6656]{1,0:T(8,128)(2,1)}), bf16[2048,6656]{1,0:T(8,128)(2,1)}) %all-gather.2.cloned.1.call-update) | async-done | bytes 27262992 | tf_op jit(solution)/shard_map/all_gather | solution.py:543
  113.1 20.0 %fusion.216 = (bf16[1024,6656]{1,0:T(8,128)(2,1)}, bf16[1024,6656]{1,0:T(8,128)(2,1)}) fusion(bf16[2048,6656]{1,0:T(8,128)(2,1)} %all-gather.2.cloned.1.call-done), kind=kLoop, calls=%fused_computation.485 | loop fusion | bytes 54525952 | tf_op jit(solution)/shard_map/slice | solution.py:550
  133.2 7.8 %slice.276 = bf16[64,16,4480]{2,1,0:T(8,128)(2,1)} slice(bf16[64,16,6656]{2,1,0:T(8,128)(2,1)} %bitcast.539), slice={[0:64], [0:16], [0:4480]} | slice | bytes 18350080 | tf_op jit(solution)/shard_map/slice | solution.py:556
  144.1 5.1 convolution_convert_fusion.3.projected
  155.3 17.9 %all_to_all.45.refs_0_ = bf16[16,144,128]{2,1,0:T(8,128)(2,1)S(1)} all-to-all(bf16[16,144,128]{2,1,0:T(8,128)(2,1)S(1)} %get-tuple-element.51), channel_id=1, replica_groups=mesh['dp'=4,'section'=2,'seq'=16] {'seq'}, dimensions={0} | all-to-all | bytes 1179648 | tf_op jit(solution)/shard_map/all_to_all | solution.py:401
  174.1 3.8 all-to-all-start.1
  177.9 4.8 slice.284
  182.7 7.7 slice.287
  191.5 7.8 %reshape.525 = bf16[64,16,2,1024]{3,2,1,0:T(2,128)(2,1)} reshape(bf16[64,16,2048]{2,1,0:T(8,128)(2,1)} %slice.284) | data formatting | bytes 8388608 | tf_op jit(solution)/shard_map/reshape | solution.py:551
  199.3 5.6 copy.66
  215.8 5.2 convolution_convert_fusion.2.projected
  230.4 7.2 all-to-all-start.2
  237.7 9.3 %all-to-all-done.2.refs_0_ = bf16[16,144,128]{2,1,0:T(8,128)(2,1)} async-done(((bf16[16,144,128]{2,1,0:T(8,128)(2,1)}), bf16[16,144,128]{2,1,0:T(8,128)(2,1)}, u32[]{:S(2)}, u32[]{:S(2)}) %all-to-all-start.2) | async-done | bytes 589856 | tf_op jit(solution)/shard_map/all_to_all | solution.py:401
  249.0 4.6 all-to-all-start.3
  253.8 4.9 slice.295
  261.2 7.8 %reshape.528 = bf16[64,16,2,1024]{3,2,1,0:T(2,128)(2,1)} reshape(bf16[64,16,2048]{2,1,0:T(8,128)(2,1)} %slice.295) | data formatting | bytes 8388608 | tf_op jit(solution)/shard_map/reshape | solution.py:551
  269.0 3.7 copy.67
  289.6 6.7 all-to-all-start.4
  300.3 5.9 collective-permute-start.3
  309.6 6.9 all-to-all-start.5
  323.2 8.7 %inner.2 = (f32[128,2048]{1,0:T(8,128)S(1)}, f32[128,256]{1,0:T(8,128)S(1)}, f32[128,128]{1,0:T(8,128)S(1)}) custom-call(f32[128,2048]{1,0:T(8,128)S(1)} %copy-done.2, bf16[128,256]{1,0:T(8,128)(2,1)S(1)} %get-tuple-element.54.bc, f32[128,128]{1,0:T(8,128)S(1)} %copy-done.45, f32[128,128]{1,0:T(8,128)S(1)} %copy-done.26, bf16[128,2048]{1,0:T(8,128)(2,1)S(1)} %copy-done.19, ...), custom_call_target="tpu_custom_call" | custom-call | tf_op jit(solution)/shard_map/inner/pallas_call | solution.py:326
  344.5 5.3 outer.2
  363.6 7.6 multiply_reduce_fusion
  377.3 7.9 %all-to-all-start.6 = ((bf16[16,144,128]{2,1,0:T(8,128)(2,1)}), bf16[16,144,128]{2,1,0:T(8,128)(2,1)}, u32[]{:S(2)}, u32[]{:S(2)}) async-start(bf16[16,144,128]{2,1,0:T(8,128)(2,1)} %copy-done.48), calls=%async_computation.6 | async-start | bytes 1179648 | tf_op jit(solution)/shard_map/all_to_all | solution.py:401
  394.2 7.6 inner.3
  414.6 6.9 all-to-all-start.7
  441.9 4.1 outer.3
  458.4 6.7 fusion.32
  465.1 5.0 convolution_convert_fusion.1
  470.3 4.9 dynamic-slice_bitcast_fusion.1
  475.6 4.6 collective-permute-start.120
  490.5 6.7 collective-permute-start.7
  515.4 6.1 collective-permute-start.36
  526.3 5.8 all-to-all-start.8
  533.0 9.7 %all-to-all-done.8 = f32[64,8,128]{2,1,0:T(8,128)S(1)} async-done(((f32[64,8,128]{2,1,0:T(8,128)}), f32[64,8,128]{2,1,0:T(8,128)S(1)}, u32[]{:S(2)}, u32[]{:S(2)}) %all-to-all-start.8) | async-done | bytes 262176 | tf_op jit(solution)/shard_map/all_to_all | solution.py:590
  569.1 4.0 collective-permute-done.77
  575.2 3.9 collective-permute-done.68
  581.2 4.7 collective-permute-start.78
  601.5 7.8 %collective-permute-start.121 = (f32[16,1024]{1,0:T(8,128)S(1)}, f32[16,1024]{1,0:T(8,128)S(1)}, u32[]{:S(2)}, u32[]{:S(2)}) collective-permute-start(f32[16,1024]{1,0:T(8,128)S(1)} %get-tuple-element.214), channel_id=1, source_target_pairs={{0,16},{16,0},{1,17},{17,1},{2,18},{18,2},{3,19},{19,3},{4,20},{20... | collective-permute-start | bytes 196616 | tf_op jit(solution)/shard_map/ppermute | solution.py:336
  619.6 9.3 %collective-permute-done.57 = bf16[4,4,8,1408]{3,2,1,0:T(8,128)(2,1)S(1)} collective-permute-done((bf16[4,4,8,1408]{3,2,1,0:T(8,128)(2,1)S(1)}, bf16[4,4,8,1408]{3,2,1,0:T(8,128)(2,1)S(1)}, u32[]{:S(2)}, u32[]{:S(2)}) %collective-permute-start.57) | collective-permute-done | bytes 360480 | tf_op jit(solution)/shard_map/ppermute | solution.py:349
  630.1 4.3 collective-permute-done.56
  641.5 5.8 collective-permute-done.38
  651.5 7.2 collective-permute-done.47
  691.1 3.6 fusion.1
  698.0 5.4 collective-permute-done.29
  728.0 6.3 collective-permute-start.22
  736.0 4.0 collective-permute-done.21
  748.7 15.3 %collective-permute-start.64 = (f32[8,4480]{1,0:T(8,128)S(1)}, f32[8,4480]{1,0:T(8,128)S(1)}, u32[]{:S(2)}, u32[]{:S(2)}) collective-permute-start(f32[8,4480]{1,0:T(8,128)S(1)} %get-tuple-element.188), channel_id=1, source_target_pairs={{0,16},{16,0},{1,17},{17,1},{2,18},{18,2},{3,19},{19,3},{4,20},{20... | collective-permute-start | bytes 430088 | tf_op jit(solution)/shard_map/ppermute | solution.py:336
  (705 shorter events, 338.6 us)
Async XLA Ops:
  7.2 106.0 %all-gather.2.cloned.1.call-start = ((), (), s32[]{:S(2)}) async-start(), calls=%async_computation.9 | async-start | bytes 27475968 | tf_op jit(solution)/shard_map/all_gather | solution.py:543
  174.1 36.0 %all-to-all-start.1 = ((bf16[16,128,128]{2,1,0:T(8,128)(2,1)}), bf16[16,128,128]{2,1,0:T(8,128)(2,1)S(1)}, u32[]{:S(2)}, u32[]{:S(2)}) async-start(bf16[16,128,128]{2,1,0:T(8,128)(2,1)} %scan.2), calls=%async_computation.1 | async-start | bytes 1048576 | tf_op jit(solution)/shard_map/all_to_all | solution.py:409
  230.4 16.7 %all-to-all-start.2 = ((bf16[16,144,128]{2,1,0:T(8,128)(2,1)}), bf16[16,144,128]{2,1,0:T(8,128)(2,1)}, u32[]{:S(2)}, u32[]{:S(2)}) async-start(bf16[16,144,128]{2,1,0:T(8,128)(2,1)} %copy-done.47), calls=%async_computation.2 | async-start | bytes 1179648 | tf_op jit(solution)/shard_map/all_to_all | solution.py:401
  249.0 28.8 %all-to-all-start.3 = ((bf16[16,128,128]{2,1,0:T(8,128)(2,1)}), bf16[16,128,128]{2,1,0:T(8,128)(2,1)}, u32[]{:S(2)}, u32[]{:S(2)}) async-start(bf16[16,128,128]{2,1,0:T(8,128)(2,1)} %copy-done.14), calls=%async_computation.3 | async-start | bytes 1048576 | tf_op jit(solution)/shard_map/all_to_all | solution.py:409
  289.6 18.1 %all-to-all-start.4 = ((bf16[16,144,128]{2,1,0:T(8,128)(2,1)}), bf16[16,144,128]{2,1,0:T(8,128)(2,1)}, u32[]{:S(2)}, u32[]{:S(2)}) async-start(bf16[16,144,128]{2,1,0:T(8,128)(2,1)} %copy-done.49), calls=%async_computation.4 | async-start | bytes 1179648 | tf_op jit(solution)/shard_map/all_to_all | solution.py:401
  300.3 33.8 %collective-permute-start.3 = (bf16[128,512]{1,0:T(8,128)(2,1)}, bf16[128,512]{1,0:T(8,128)(2,1)}, u32[]{:S(2)}, u32[]{:S(2)}) collective-permute-start(bf16[128,512]{1,0:T(8,128)(2,1)} %get-tuple-element.174), channel_id=1, source_target_pairs={{0,16},{16,0},{1,17},{17,1},{2,18},{18,2},{3,19},{19,3},{4,20},{20... | collective-permute-start | bytes 393224 | tf_op jit(solution)/shard_map/ppermute | solution.py:336
  309.6 26.2 %all-to-all-start.5 = ((bf16[16,128,128]{2,1,0:T(8,128)(2,1)}), bf16[16,128,128]{2,1,0:T(8,128)(2,1)}, u32[]{:S(2)}, u32[]{:S(2)}) async-start(bf16[16,128,128]{2,1,0:T(8,128)(2,1)} %copy-done.21), calls=%async_computation.5 | async-start | bytes 1048576 | tf_op jit(solution)/shard_map/all_to_all | solution.py:409
  320.6 100.9 %collective-permute-start.93 = (bf16[64,16,1024]{2,1,0:T(8,128)(2,1)}, bf16[64,16,1024]{2,1,0:T(8,128)(2,1)}, u32[]{:S(2)}, u32[]{:S(2)}) collective-permute-start(bf16[64,16,1024]{2,1,0:T(8,128)(2,1)} %dynamic-slice_bitcast_fusion.2), channel_id=1, source_target_pairs={{0,16},{16,0},{1,17},{17,1},{2,18},{18,2},{3,19},{19,3},{4,20},{20... | collective-permute-start | bytes 6291464 | tf_op jit(solution)/shard_map/ppermute | solution.py:336
  377.3 35.4 %all-to-all-start.6 = ((bf16[16,144,128]{2,1,0:T(8,128)(2,1)}), bf16[16,144,128]{2,1,0:T(8,128)(2,1)}, u32[]{:S(2)}, u32[]{:S(2)}) async-start(bf16[16,144,128]{2,1,0:T(8,128)(2,1)} %copy-done.48), calls=%async_computation.6 | async-start | bytes 1179648 | tf_op jit(solution)/shard_map/all_to_all | solution.py:401
  391.4 151.9 %collective-permute-start.65 = (bf16[64,16,1024]{2,1,0:T(8,128)(2,1)}, bf16[64,16,1024]{2,1,0:T(8,128)(2,1)}, u32[]{:S(2)}, u32[]{:S(2)}) collective-permute-start(bf16[64,16,1024]{2,1,0:T(8,128)(2,1)} %dynamic-slice_bitcast_fusion.3), channel_id=1, source_target_pairs={{0,16},{16,0},{1,17},{17,1},{2,18},{18,2},{3,19},{19,3},{4,20},{20... | collective-permute-start | bytes 6291464 | tf_op jit(solution)/shard_map/ppermute | solution.py:336
  414.6 22.3 %all-to-all-start.7 = ((bf16[16,128,128]{2,1,0:T(8,128)(2,1)}), bf16[16,128,128]{2,1,0:T(8,128)(2,1)S(1)}, u32[]{:S(2)}, u32[]{:S(2)}) async-start(bf16[16,128,128]{2,1,0:T(8,128)(2,1)} %scan_back.3), calls=%async_computation.7 | async-start | bytes 1048576 | tf_op jit(solution)/shard_map/all_to_all | solution.py:409
  425.7 23.7 %collective-permute-start.114 = (bf16[4,4,16,256]{3,2,1,0:T(8,128)(2,1)}, bf16[4,4,16,256]{3,2,1,0:T(8,128)(2,1)}, u32[]{:S(2)}, u32[]{:S(2)}) collective-permute-start(bf16[4,4,16,256]{3,2,1,0:T(8,128)(2,1)} %get-tuple-element.154), channel_id=1, source_target_pairs={{0,2},{1,3},{2,0},{3,1},{4,6},{5,7},{6,4},{7,5},{8,10},{9,11},{10,... | collective-permute-start | bytes 393224 | tf_op jit(solution)/shard_map/ppermute | solution.py:349
  428.6 22.1 %collective-permute-start.113 = (bf16[4,4,16,256]{3,2,1,0:T(8,128)(2,1)}, bf16[4,4,16,256]{3,2,1,0:T(8,128)(2,1)}, u32[]{:S(2)}, u32[]{:S(2)}) collective-permute-start(bf16[4,4,16,256]{3,2,1,0:T(8,128)(2,1)} %get-tuple-element.153), channel_id=1, source_target_pairs={{0,3},{1,0},{2,1},{3,2},{4,7},{5,4},{6,5},{7,6},{8,11},{9,8},{10,9... | collective-permute-start | bytes 393224 | tf_op jit(solution)/shard_map/ppermute | solution.py:349
  429.4 21.2 %collective-permute-start.112 = (bf16[4,4,16,256]{3,2,1,0:T(8,128)(2,1)}, bf16[4,4,16,256]{3,2,1,0:T(8,128)(2,1)}, u32[]{:S(2)}, u32[]{:S(2)}) collective-permute-start(bf16[4,4,16,256]{3,2,1,0:T(8,128)(2,1)} %get-tuple-element.152), channel_id=1, source_target_pairs={{0,1},{1,2},{2,3},{3,0},{4,5},{5,6},{6,7},{7,4},{8,9},{9,10},{10,1... | collective-permute-start | bytes 393224 | tf_op jit(solution)/shard_map/ppermute | solution.py:349
  431.9 56.4 %collective-permute-start.105 = (bf16[4,4,16,384]{3,2,0,1:T(8,128)(2,1)}, bf16[4,4,16,384]{3,2,0,1:T(8,128)(2,1)}, u32[]{:S(2)}, u32[]{:S(2)}) collective-permute-start(bf16[4,4,16,384]{3,2,0,1:T(8,128)(2,1)} %bitcast.527), channel_id=1, source_target_pairs={{0,8},{1,9},{2,10},{3,11},{4,12},{5,13},{6,14},{7,15},{8,0},{9,1},... | collective-permute-start | bytes 589832 | tf_op jit(solution)/shard_map/ppermute | solution.py:349
  451.9 23.7 %collective-permute-start.117 = (bf16[4,16,256]{2,1,0:T(8,128)(2,1)S(1)}, bf16[4,16,256]{2,1,0:T(8,128)(2,1)S(1)}, u32[]{:S(2)}, u32[]{:S(2)}) collective-permute-start(bf16[4,16,256]{2,1,0:T(8,128)(2,1)S(1)} %get-tuple-element.193), channel_id=1, source_target_pairs={{0,64},{32,96},{64,0},{96,32},{1,65},{33,97},{65,1},{97,33},{2,66}... | collective-permute-start | bytes 98312 | tf_op jit(solution)/shard_map/ppermute | solution.py:341
  453.0 22.5 %collective-permute-start.116 = (bf16[4,16,256]{2,1,0:T(8,128)(2,1)S(1)}, bf16[4,16,256]{2,1,0:T(8,128)(2,1)S(1)}, u32[]{:S(2)}, u32[]{:S(2)}) collective-permute-start(bf16[4,16,256]{2,1,0:T(8,128)(2,1)S(1)} %get-tuple-element.194), channel_id=1, source_target_pairs={{0,96},{32,0},{64,32},{96,64},{1,97},{33,1},{65,33},{97,65},{2,98}... | collective-permute-start | bytes 98312 | tf_op jit(solution)/shard_map/ppermute | solution.py:341
  454.5 21.1 %collective-permute-start.115 = (bf16[4,16,256]{2,1,0:T(8,128)(2,1)S(1)}, bf16[4,16,256]{2,1,0:T(8,128)(2,1)S(1)}, u32[]{:S(2)}, u32[]{:S(2)}) collective-permute-start(bf16[4,16,256]{2,1,0:T(8,128)(2,1)S(1)} %get-tuple-element.192), channel_id=1, source_target_pairs={{0,32},{32,64},{64,96},{96,0},{1,33},{33,65},{65,97},{97,1},{2,34}... | collective-permute-start | bytes 98312 | tf_op jit(solution)/shard_map/ppermute | solution.py:341
  486.0 12.3 %collective-permute-start.96 = (bf16[4,4,16,384]{3,2,1,0:T(8,128)(2,1)S(1)}, bf16[4,4,16,384]{3,2,1,0:T(8,128)(2,1)S(1)}, u32[]{:S(2)}, u32[]{:S(2)}) collective-permute-start(bf16[4,4,16,384]{3,2,1,0:T(8,128)(2,1)S(1)} %copy-done.105), channel_id=1, source_target_pairs={{0,64},{32,96},{64,0},{96,32},{1,65},{33,97},{65,1},{97,33},{2,66}... | collective-permute-start | bytes 589832 | tf_op jit(solution)/shard_map/ppermute | solution.py:341
  488.4 10.1 %collective-permute-start.95 = (bf16[4,4,16,384]{3,2,1,0:T(8,128)(2,1)S(1)}, bf16[4,4,16,384]{3,2,1,0:T(8,128)(2,1)S(1)}, u32[]{:S(2)}, u32[]{:S(2)}) collective-permute-start(bf16[4,4,16,384]{3,2,1,0:T(8,128)(2,1)S(1)} %copy-done.104), channel_id=1, source_target_pairs={{0,96},{32,0},{64,32},{96,64},{1,97},{33,1},{65,33},{97,65},{2,98}... | collective-permute-start | bytes 589832 | tf_op jit(solution)/shard_map/ppermute | solution.py:341
  489.3 10.0 %collective-permute-start.94 = (bf16[4,4,16,384]{3,2,1,0:T(8,128)(2,1)S(1)}, bf16[4,4,16,384]{3,2,1,0:T(8,128)(2,1)S(1)}, u32[]{:S(2)}, u32[]{:S(2)}) collective-permute-start(bf16[4,4,16,384]{3,2,1,0:T(8,128)(2,1)S(1)} %copy-done.103), channel_id=1, source_target_pairs={{0,32},{32,64},{64,96},{96,0},{1,33},{33,65},{65,97},{97,1},{2,34}... | collective-permute-start | bytes 589832 | tf_op jit(solution)/shard_map/ppermute | solution.py:341
  490.5 33.8 %collective-permute-start.7 = (f32[64,8,128]{2,0,1:T(8,128)S(1)}, f32[64,8,128]{2,0,1:T(8,128)S(1)}, u32[]{:S(2)}, u32[]{:S(2)}) collective-permute-start(f32[64,8,128]{2,0,1:T(8,128)S(1)} %broadcast_select_fusion), channel_id=1, source_target_pairs={{0,16},{16,0},{1,17},{17,1},{2,18},{18,2},{3,19},{19,3},{4,20},{20... | collective-permute-start | bytes 786440 | tf_op jit(solution)/shard_map/ppermute | solution.py:336
  512.5 9.0 %collective-permute-start.101 = (bf16[16,384]{1,0:T(8,128)(2,1)S(1)}, bf16[16,384]{1,0:T(8,128)(2,1)S(1)}, u32[]{:S(2)}, u32[]{:S(2)}) collective-permute-start(bf16[16,384]{1,0:T(8,128)(2,1)S(1)} %get-tuple-element.225), channel_id=1, source_target_pairs={{0,3},{1,0},{2,1},{3,2},{4,7},{5,4},{6,5},{7,6},{8,11},{9,8},{10,9... | collective-permute-start | bytes 36872 | tf_op jit(solution)/shard_map/ppermute | solution.py:349
  515.4 93.9 %collective-permute-start.36 = (bf16[64,8,4480]{2,1,0:T(8,128)(2,1)}, bf16[64,8,4480]{2,1,0:T(8,128)(2,1)}, u32[]{:S(2)}, u32[]{:S(2)}) collective-permute-start(bf16[64,8,4480]{2,1,0:T(8,128)(2,1)} %dynamic-slice_bitcast_fusion), channel_id=1, source_target_pairs={{0,16},{16,0},{1,17},{17,1},{2,18},{18,2},{3,19},{19,3},{4,20},{20... | collective-permute-start | bytes 13762568 | tf_op jit(solution)/shard_map/ppermute | solution.py:336
  521.6 10.6 %collective-permute-start.6 = (bf16[128,512]{1,0:T(8,128)(2,1)S(1)}, bf16[128,512]{1,0:T(8,128)(2,1)S(1)}, u32[]{:S(2)}, u32[]{:S(2)}) collective-permute-start(bf16[128,512]{1,0:T(8,128)(2,1)S(1)} %select_convert_fusion), channel_id=1, source_target_pairs={{0,16},{16,0},{1,17},{17,1},{2,18},{18,2},{3,19},{19,3},{4,20},{20... | collective-permute-start | bytes 393224 | tf_op jit(solution)/shard_map/ppermute | solution.py:336
  521.6 169.5 %collective-permute-start.8 = (bf16[64,8,4480]{2,1,0:T(8,128)(2,1)}, bf16[64,8,4480]{2,1,0:T(8,128)(2,1)}, u32[]{:S(2)}, u32[]{:S(2)}) collective-permute-start(bf16[64,8,4480]{2,1,0:T(8,128)(2,1)} %dynamic-slice_bitcast_fusion.1), channel_id=1, source_target_pairs={{0,16},{16,0},{1,17},{17,1},{2,18},{18,2},{3,19},{19,3},{4,20},{20... | collective-permute-start | bytes 13762568 | tf_op jit(solution)/shard_map/ppermute | solution.py:336
  526.3 16.4 %all-to-all-start.8 = ((f32[64,8,128]{2,1,0:T(8,128)}), f32[64,8,128]{2,1,0:T(8,128)S(1)}, u32[]{:S(2)}, u32[]{:S(2)}) async-start(f32[64,8,128]{2,1,0:T(8,128)} %copy.68), calls=%async_computation.8 | async-start | bytes 524288 | tf_op jit(solution)/shard_map/all_to_all | solution.py:590
  601.5 164.2 %collective-permute-start.121 = (f32[16,1024]{1,0:T(8,128)S(1)}, f32[16,1024]{1,0:T(8,128)S(1)}, u32[]{:S(2)}, u32[]{:S(2)}) collective-permute-start(f32[16,1024]{1,0:T(8,128)S(1)} %get-tuple-element.214), channel_id=1, source_target_pairs={{0,16},{16,0},{1,17},{17,1},{2,18},{18,2},{3,19},{19,3},{4,20},{20... | collective-permute-start | bytes 196616 | tf_op jit(solution)/shard_map/ppermute | solution.py:336
  617.3 11.7 %collective-permute-start.57 = (bf16[4,4,8,1408]{3,2,1,0:T(8,128)(2,1)S(1)}, bf16[4,4,8,1408]{3,2,1,0:T(8,128)(2,1)S(1)}, u32[]{:S(2)}, u32[]{:S(2)}) collective-permute-start(bf16[4,4,8,1408]{3,2,1,0:T(8,128)(2,1)S(1)} %get-tuple-element.135), channel_id=1, source_target_pairs={{0,2},{1,3},{2,0},{3,1},{4,6},{5,7},{6,4},{7,5},{8,10},{9,11},{10,... | collective-permute-start | bytes 1081352 | tf_op jit(solution)/shard_map/ppermute | solution.py:349
  617.4 17.0 %collective-permute-start.56 = (bf16[4,4,8,1408]{3,2,1,0:T(8,128)(2,1)S(1)}, bf16[4,4,8,1408]{3,2,1,0:T(8,128)(2,1)S(1)}, u32[]{:S(2)}, u32[]{:S(2)}) collective-permute-start(bf16[4,4,8,1408]{3,2,1,0:T(8,128)(2,1)S(1)} %get-tuple-element.134), channel_id=1, source_target_pairs={{0,3},{1,0},{2,1},{3,2},{4,7},{5,4},{6,5},{7,6},{8,11},{9,8},{10,9... | collective-permute-start | bytes 1081352 | tf_op jit(solution)/shard_map/ppermute | solution.py:349
  619.3 17.6 %collective-permute-start.55 = (bf16[4,4,8,1408]{3,2,1,0:T(8,128)(2,1)S(1)}, bf16[4,4,8,1408]{3,2,1,0:T(8,128)(2,1)S(1)}, u32[]{:S(2)}, u32[]{:S(2)}) collective-permute-start(bf16[4,4,8,1408]{3,2,1,0:T(8,128)(2,1)S(1)} %get-tuple-element.133), channel_id=1, source_target_pairs={{0,1},{1,2},{2,3},{3,0},{4,5},{5,6},{6,7},{7,4},{8,9},{9,10},{10,1... | collective-permute-start | bytes 1081352 | tf_op jit(solution)/shard_map/ppermute | solution.py:349
  629.0 10.9 %collective-permute-start.39 = (bf16[4,4,8,1536]{3,2,1,0:T(8,128)(2,1)S(1)}, bf16[4,4,8,1536]{3,2,1,0:T(8,128)(2,1)S(1)}, u32[]{:S(2)}, u32[]{:S(2)}) collective-permute-start(bf16[4,4,8,1536]{3,2,1,0:T(8,128)(2,1)S(1)} %get-tuple-element.124), channel_id=1, source_target_pairs={{0,64},{32,96},{64,0},{96,32},{1,65},{33,97},{65,1},{97,33},{2,66}... | collective-permute-start | bytes 1179656 | tf_op jit(solution)/shard_map/ppermute | solution.py:341
  634.4 12.9 %collective-permute-start.38 = (bf16[4,4,8,1536]{3,2,1,0:T(8,128)(2,1)S(1)}, bf16[4,4,8,1536]{3,2,1,0:T(8,128)(2,1)S(1)}, u32[]{:S(2)}, u32[]{:S(2)}) collective-permute-start(bf16[4,4,8,1536]{3,2,1,0:T(8,128)(2,1)S(1)} %get-tuple-element.125), channel_id=1, source_target_pairs={{0,96},{32,0},{64,32},{96,64},{1,97},{33,1},{65,33},{97,65},{2,98}... | collective-permute-start | bytes 1179656 | tf_op jit(solution)/shard_map/ppermute | solution.py:341
  636.9 12.9 %collective-permute-start.37 = (bf16[4,4,8,1536]{3,2,1,0:T(8,128)(2,1)S(1)}, bf16[4,4,8,1536]{3,2,1,0:T(8,128)(2,1)S(1)}, u32[]{:S(2)}, u32[]{:S(2)}) collective-permute-start(bf16[4,4,8,1536]{3,2,1,0:T(8,128)(2,1)S(1)} %get-tuple-element.123), channel_id=1, source_target_pairs={{0,32},{32,64},{64,96},{96,0},{1,33},{33,65},{65,97},{97,1},{2,34}... | collective-permute-start | bytes 1179656 | tf_op jit(solution)/shard_map/ppermute | solution.py:341
  639.9 10.5 %collective-permute-start.48 = (bf16[4,4,8,1536]{3,2,0,1:T(8,128)(2,1)S(1)}, bf16[4,4,8,1536]{3,2,0,1:T(8,128)(2,1)S(1)}, u32[]{:S(2)}, u32[]{:S(2)}) collective-permute-start(bf16[4,4,8,1536]{3,2,0,1:T(8,128)(2,1)S(1)} %bitcast.572), channel_id=1, source_target_pairs={{0,8},{1,9},{2,10},{3,11},{4,12},{5,13},{6,14},{7,15},{8,0},{9,1},... | collective-permute-start | bytes 1179656 | tf_op jit(solution)/shard_map/ppermute | solution.py:349
  647.3 11.4 %collective-permute-start.47 = (bf16[4,4,8,1536]{3,2,0,1:T(8,128)(2,1)S(1)}, bf16[4,4,8,1536]{3,2,0,1:T(8,128)(2,1)S(1)}, u32[]{:S(2)}, u32[]{:S(2)}) collective-permute-start(bf16[4,4,8,1536]{3,2,0,1:T(8,128)(2,1)S(1)} %bitcast.571), channel_id=1, source_target_pairs={{0,12},{1,13},{2,14},{3,15},{4,0},{5,1},{6,2},{7,3},{8,4},{9,5},{1... | collective-permute-start | bytes 1179656 | tf_op jit(solution)/shard_map/ppermute | solution.py:349
  649.9 11.3 %collective-permute-start.46 = (bf16[4,4,8,1536]{3,2,0,1:T(8,128)(2,1)S(1)}, bf16[4,4,8,1536]{3,2,0,1:T(8,128)(2,1)S(1)}, u32[]{:S(2)}, u32[]{:S(2)}) collective-permute-start(bf16[4,4,8,1536]{3,2,0,1:T(8,128)(2,1)S(1)} %bitcast.570), channel_id=1, source_target_pairs={{0,4},{1,5},{2,6},{3,7},{4,8},{5,9},{6,10},{7,11},{8,12},{9,13},{1... | collective-permute-start | bytes 1179656 | tf_op jit(solution)/shard_map/ppermute | solution.py:349
  650.4 12.3 %collective-permute-start.60 = (bf16[4,8,1408]{2,1,0:T(8,128)(2,1)S(1)}, bf16[4,8,1408]{2,1,0:T(8,128)(2,1)S(1)}, u32[]{:S(2)}, u32[]{:S(2)}) collective-permute-start(bf16[4,8,1408]{2,1,0:T(8,128)(2,1)S(1)} %get-tuple-element.171), channel_id=1, source_target_pairs={{0,64},{32,96},{64,0},{96,32},{1,65},{33,97},{65,1},{97,33},{2,66}... | collective-permute-start | bytes 270344 | tf_op jit(solution)/shard_map/ppermute | solution.py:341
  695.5 9.7 %collective-permute-start.28 = (bf16[4,4,8,1408]{3,2,1,0:T(8,128)(2,1)S(1)}, bf16[4,4,8,1408]{3,2,1,0:T(8,128)(2,1)S(1)}, u32[]{:S(2)}, u32[]{:S(2)}) collective-permute-start(bf16[4,4,8,1408]{3,2,1,0:T(8,128)(2,1)S(1)} %get-tuple-element.132), channel_id=1, source_target_pairs={{0,3},{1,0},{2,1},{3,2},{4,7},{5,4},{6,5},{7,6},{8,11},{9,8},{10,9... | collective-permute-start | bytes 1081352 | tf_op jit(solution)/shard_map/ppermute | solution.py:349
  696.6 10.5 %collective-permute-start.27 = (bf16[4,4,8,1408]{3,2,1,0:T(8,128)(2,1)S(1)}, bf16[4,4,8,1408]{3,2,1,0:T(8,128)(2,1)S(1)}, u32[]{:S(2)}, u32[]{:S(2)}) collective-permute-start(bf16[4,4,8,1408]{3,2,1,0:T(8,128)(2,1)S(1)} %get-tuple-element.130), channel_id=1, source_target_pairs={{0,1},{1,2},{2,3},{3,0},{4,5},{5,6},{6,7},{7,4},{8,9},{9,10},{10,1... | collective-permute-start | bytes 1081352 | tf_op jit(solution)/shard_map/ppermute | solution.py:349
  697.1 10.3 %collective-permute-start.20 = (bf16[4,4,8,1536]{3,2,1,0:T(8,128)(2,1)S(1)}, bf16[4,4,8,1536]{3,2,1,0:T(8,128)(2,1)S(1)}, u32[]{:S(2)}, u32[]{:S(2)}) collective-permute-start(bf16[4,4,8,1536]{3,2,1,0:T(8,128)(2,1)S(1)} %get-tuple-element.121), channel_id=1, source_target_pairs={{0,8},{1,9},{2,10},{3,11},{4,12},{5,13},{6,14},{7,15},{8,0},{9,1},... | collective-permute-start | bytes 1179656 | tf_op jit(solution)/shard_map/ppermute | solution.py:349
  705.2 8.5 %collective-permute-start.18 = (bf16[4,4,8,1536]{3,2,1,0:T(8,128)(2,1)S(1)}, bf16[4,4,8,1536]{3,2,1,0:T(8,128)(2,1)S(1)}, u32[]{:S(2)}, u32[]{:S(2)}) collective-permute-start(bf16[4,4,8,1536]{3,2,1,0:T(8,128)(2,1)S(1)} %get-tuple-element.120), channel_id=1, source_target_pairs={{0,4},{1,5},{2,6},{3,7},{4,8},{5,9},{6,10},{7,11},{8,12},{9,13},{1... | collective-permute-start | bytes 1179656 | tf_op jit(solution)/shard_map/ppermute | solution.py:349
  707.1 8.4 %collective-permute-start.11 = (bf16[4,4,8,1536]{3,2,1,0:T(8,128)(2,1)S(1)}, bf16[4,4,8,1536]{3,2,1,0:T(8,128)(2,1)S(1)}, u32[]{:S(2)}, u32[]{:S(2)}) collective-permute-start(bf16[4,4,8,1536]{3,2,1,0:T(8,128)(2,1)S(1)} %get-tuple-element.118), channel_id=1, source_target_pairs={{0,64},{32,96},{64,0},{96,32},{1,65},{33,97},{65,1},{97,33},{2,66}... | collective-permute-start | bytes 1179656 | tf_op jit(solution)/shard_map/ppermute | solution.py:341
  707.4 11.1 %collective-permute-start.10 = (bf16[4,4,8,1536]{3,2,1,0:T(8,128)(2,1)S(1)}, bf16[4,4,8,1536]{3,2,1,0:T(8,128)(2,1)S(1)}, u32[]{:S(2)}, u32[]{:S(2)}) collective-permute-start(bf16[4,4,8,1536]{3,2,1,0:T(8,128)(2,1)S(1)} %get-tuple-element.119), channel_id=1, source_target_pairs={{0,96},{32,0},{64,32},{96,64},{1,97},{33,1},{65,33},{97,65},{2,98}... | collective-permute-start | bytes 1179656 | tf_op jit(solution)/shard_map/ppermute | solution.py:341
  710.3 9.2 %collective-permute-start.9 = (bf16[4,4,8,1536]{3,2,1,0:T(8,128)(2,1)S(1)}, bf16[4,4,8,1536]{3,2,1,0:T(8,128)(2,1)S(1)}, u32[]{:S(2)}, u32[]{:S(2)}) collective-permute-start(bf16[4,4,8,1536]{3,2,1,0:T(8,128)(2,1)S(1)} %get-tuple-element.117), channel_id=1, source_target_pairs={{0,32},{32,64},{64,96},{96,0},{1,33},{33,65},{65,97},{97,1},{2,34}... | collective-permute-start | bytes 1179656 | tf_op jit(solution)/shard_map/ppermute | solution.py:341
  719.5 15.0 %collective-permute-start.23 = (bf16[4,8,1536]{2,1,0:T(8,128)(2,1)S(1)}, bf16[4,8,1536]{2,1,0:T(8,128)(2,1)S(1)}, u32[]{:S(2)}, u32[]{:S(2)}) collective-permute-start(bf16[4,8,1536]{2,1,0:T(8,128)(2,1)S(1)} %get-tuple-element.159), channel_id=1, source_target_pairs={{0,2},{1,3},{2,0},{3,1},{4,6},{5,7},{6,4},{7,5},{8,10},{9,11},{10,... | collective-permute-start | bytes 294920 | tf_op jit(solution)/shard_map/ppermute | solution.py:349
  723.7 10.6 %collective-permute-start.34 = (bf16[8,1408]{1,0:T(8,128)(2,1)S(1)}, bf16[8,1408]{1,0:T(8,128)(2,1)S(1)}, u32[]{:S(2)}, u32[]{:S(2)}) collective-permute-start(bf16[8,1408]{1,0:T(8,128)(2,1)S(1)} %get-tuple-element.209), channel_id=1, source_target_pairs={{0,12},{1,13},{2,14},{3,15},{4,0},{5,1},{6,2},{7,3},{8,4},{9,5},{1... | collective-permute-start | bytes 67592 | tf_op jit(solution)/shard_map/ppermute | solution.py:349
  748.7 17.6 %collective-permute-start.64 = (f32[8,4480]{1,0:T(8,128)S(1)}, f32[8,4480]{1,0:T(8,128)S(1)}, u32[]{:S(2)}, u32[]{:S(2)}) collective-permute-start(f32[8,4480]{1,0:T(8,128)S(1)} %get-tuple-element.188), channel_id=1, source_target_pairs={{0,16},{16,0},{1,17},{17,1},{2,18},{18,2},{3,19},{19,3},{4,20},{20... | collective-permute-start | bytes 430088 | tf_op jit(solution)/shard_map/ppermute | solution.py:336
  (209 other events, 2060.2 us)
Sparse Core Ops, SparseCore 0:
  12.6 100.5 all-gather.1
